TPU v7x, 32 devices: a whole 2x2x4 slice. The times are simulated.
32 devices in a mesh: fsdp: 8 (over z, x), dp: 4 (over y, core).
Axes of the slice: x: 2, y: 2, z: 4, core: 2. Of those that a mesh axis runs over, the one named last changes fastest.
Arguments:
- hidden_in: bfloat16 [64, 512, 1088], P(('fsdp', 'dp')), may hold values from -6 to 6
- cotangent: bfloat16 [64, 512, 1088], P(('fsdp', 'dp')), may hold values from -6 to 6
- lengths: int32 [64], P(('fsdp', 'dp')), may hold values from 1 to 512, as said below
- qkv_weight: float32 [1088, 3264], P('fsdp'), may hold values from -0.1875 to 0.1875
- qkv_mean: float32 [1088, 3264], P('fsdp'), may hold values from -40 to 40
- qkv_square: float32 [1088, 3264], P('fsdp'), may hold values from 3.41325 to 13.653
- out_weight: float32 [1088, 1088], P('fsdp'), may hold values from -0.75 to 0.75
- out_mean: float32 [1088, 1088], P('fsdp'), may hold values from -12 to 12
- out_square: float32 [1088, 1088], P('fsdp'), may hold values from 0.314019 to 1.22877
- up_weight: float32 [1088, 4352], P(None, 'fsdp'), may hold values from -0.1875 to 0.1875
- up_mean: float32 [1088, 4352], P(None, 'fsdp'), may hold values from -24 to 24
- up_square: float32 [1088, 4352], P(None, 'fsdp'), may hold values from 1.22877 to 4.91508
- down_weight: float32 [4352, 1088], P('fsdp'), may hold values from -0.09375 to 0.09375
- down_mean: float32 [4352, 1088], P('fsdp'), may hold values from -48 to 48
- down_square: float32 [4352, 1088], P('fsdp'), may hold values from 5.73426 to 23.2101
- vectors: float32 [8, 1088], P(None, 'fsdp'), may hold values from -1.2 to 1.4, as said below
- vectors_mean: float32 [8, 1088], P(None, 'fsdp'), may hold values from -64 to 64
- vectors_square: float32 [8, 1088], P(None, 'fsdp'), may hold values from 8.73792 to 35.4978
- upbias: float32 [4352], P('fsdp'), may hold values from -1.25 to 1.25
- upbias_mean: float32 [4352], P('fsdp'), may hold values from -24 to 24
- upbias_square: float32 [4352], P('fsdp'), may hold values from 1.22877 to 4.91508
Outputs:
- output: bfloat16 [64, 512, 1088], P(('fsdp', 'dp'))
- input_grad: float32 [64, 512, 1088], P(('fsdp', 'dp'))
- qkv_next: float32 [1088, 3264], P('fsdp')
- qkvmean_next: float32 [1088, 3264], P('fsdp')
- qkvsquare_next: float32 [1088, 3264], P('fsdp')
- out_next: float32 [1088, 1088], P('fsdp')
- outmean_next: float32 [1088, 1088], P('fsdp')
- outsquare_next: float32 [1088, 1088], P('fsdp')
- up_next: float32 [1088, 4352], P(None, 'fsdp')
- upmean_next: float32 [1088, 4352], P(None, 'fsdp')
- upsquare_next: float32 [1088, 4352], P(None, 'fsdp')
- down_next: float32 [4352, 1088], P('fsdp')
- downmean_next: float32 [4352, 1088], P('fsdp')
- downsquare_next: float32 [4352, 1088], P('fsdp')
- vectors_next: float32 [8, 1088], P(None, 'fsdp')
- vectorsmean_next: float32 [8, 1088], P(None, 'fsdp')
- vectorssquare_next: float32 [8, 1088], P(None, 'fsdp')
- upbias_next: float32 [4352], P('fsdp')
- upbiasmean_next: float32 [4352], P('fsdp')
- upbiassquare_next: float32 [4352], P('fsdp')
Inputs may be any that keep to these rules, and one draw needn't show every extreme that they name: `lengths`: every block holds one sequence of 1 to 512 tokens at its start; some block holds exactly 512. `vectors`: rows 0 and 5 are positive gains; the other rows are biases of both signs.
All inputs are finite; a program needn't handle non-finite values.
Results may differ from a plain program's by a relative error of at most 0.0095.
The roundings to bfloat16 on the way count: a program that leaves them out, or rounds other values in their place, can miss the bound.
Values may be sent and summed in bfloat16 or wider, within the bound.
No kernel may reach another device: no remote copies, remote signals or barrier semaphores. Data moves between devices by JAX's collectives and lax.ppermute only.
A program may use at most 320 MiB of HBM per device.

v0:
```python
import functools
import math

import jax
import jax.numpy as jnp
from jax import lax
from jax.experimental import pallas as pl
from jax.experimental.pallas import tpu as pltpu
from jax.sharding import PartitionSpec as P

D = 1088
HEADS = 17
HDIM = 64
BLOCK = 512
STEP = 10
EXTRA = 8

norm_eps = 1e-05
beta_first = 0.9
beta_second = 0.999
adam_floor = 1e-08
step_rates = (0.05, 0.2, 0.05, 0.03, 0.5, 0.3)
decay_rates = (0.1, 0.1, 0.1, 0.1, 0.0, 0.0)

AXES = ("fsdp", "dp")
VMEM_LIMIT = 56 * 1024 * 1024
f32 = jnp.float32
bf16 = jnp.bfloat16


class Grid:
    def __init__(self):
        self.shards = lax.axis_size("fsdp")
        self.replicas = lax.axis_size("dp")
        self.zs = self.shards // 2
        self.ys = self.replicas // 2
        f, r = lax.axis_index("fsdp"), lax.axis_index("dp")
        self.z, self.x = f // 2, f % 2
        self.y, self.c = r // 2, r % 2
        self.r = r

    def move(self, value, route):
        pairs = []
        for z in range(self.zs):
            for x in range(2):
                for y in range(2):
                    for c in range(2):
                        to_z, to_x, to_y, to_c = route(z, x, y, c)
                        here = (2 * z + x) * 4 + 2 * y + c
                        pairs.append((here, (2 * to_z + to_x) * 4 + 2 * to_y + to_c))
        return lax.ppermute(value, AXES, pairs)


def over_z(bit):
    return lambda z, x, y, c: (z ^ bit, x, y, c)


def over_x(z, x, y, c):
    return (z, 1 - x, y, c)


def over_y(z, x, y, c):
    return (z, x, 1 - y, c)


def over_core(z, x, y, c):
    return (z, x, y, 1 - c)


def x_then_y(z, x, y, c):
    return (z, 1 - x, y, c) if c == 0 else (z, x, 1 - y, c)


def y_then_x(z, x, y, c):
    return (z, x, 1 - y, c) if c == 0 else (z, 1 - x, y, c)


def after(value, *others):
    return lax.optimization_barrier((value,) + others)[0]


def take(value, at, axis=0):
    return lax.dynamic_index_in_dim(value, at, axis, keepdims=False)


def z_bits(zs):
    return [1 << i for i in range(zs.bit_length() - 1)]


def gather_z(grid, unit):
    held, off = unit[None], [0]
    for bit in reversed(z_bits(grid.zs)[1:]):
        held = jnp.concatenate([held, grid.move(held, over_z(bit))])
        off = off + [z ^ bit for z in off]
    return [held, grid.move(held, over_z(1))], [off, [z ^ 1 for z in off]]


def gather_xy(grid, held):
    both = jnp.stack([held, grid.move(held, y_then_x)])
    return [both, grid.move(both, x_then_y)]


def gather_rest(grid, halves):
    pieces = [p for held in halves for p in gather_xy(grid, held)]
    return pieces, pieces + [grid.move(p, over_core) for p in pieces]


def assemble_kernel(zs, offs, *refs):
    count = 4 * len(offs)
    pieces, (out, held, in_sems, out_sem) = refs[:count], refs[count:]
    f, r = lax.axis_index("fsdp"), lax.axis_index("dp")
    z, x, y, c = f // 2, f % 2, r // 2, r % 2
    first, second = [], []
    for number in range(count):
        dc, late = number // (count // 2), number % 2
        off = offs[(number // 2) % len(offs)]
        core = c ^ dc
        for early in range(2):
            dx = late + core * (early - late)
            dy = early + core * (late - early)
            owner = 2 * (y ^ dy) + core
            for k in range(len(off)):
                place = (owner, 2 * (z ^ off[k]) + (x ^ dx))
                sem = in_sems.at[number]
                first.append(pltpu.make_async_copy(pieces[number].at[early, k], held.at[place], sem))
                second.append(pltpu.make_async_copy(held.at[place], out.at[place], out_sem))
    for copy in first:
        copy.start()
    each = len(first) // count
    for number in range(count):
        for copy in first[number * each : (number + 1) * each]:
            copy.wait()
        for copy in second[number * each : (number + 1) * each]:
            copy.start()
    for copy in second:
        copy.wait()


def assemble(grid, pieces, offs, rows):
    whole = (4, grid.shards, rows, D)
    return pl.pallas_call(
        functools.partial(assemble_kernel, grid.zs, offs),
        out_shape=jax.ShapeDtypeStruct(whole, bf16),
        in_specs=[pl.BlockSpec(memory_space=pl.ANY)] * len(pieces),
        out_specs=pl.BlockSpec(memory_space=pl.ANY),
        scratch_shapes=[
            pltpu.VMEM(whole, bf16),
            pltpu.SemaphoreType.DMA((len(pieces),)),
            pltpu.SemaphoreType.DMA(()),
        ],
        compiler_params=pltpu.CompilerParams(vmem_limit_bytes=VMEM_LIMIT),
        cost_estimate=pl.CostEstimate(flops=0, bytes_accessed=20_000_000, transcendentals=0),
        name="assemble",
    )(*pieces)


def add(first, second):
    return (first.astype(f32) + second.astype(f32)).astype(bf16)


class Reduction:
    def __init__(self, grid, theirs, mine):
        self.grid, self.n = grid, mine.shape[2]
        self.stage = 0
        self.bits = z_bits(grid.zs)
        self.keep, self.sent = mine, theirs
        self.route = over_core

    def step(self):
        grid, n = self.grid, self.n
        total = add(self.keep, grid.move(self.sent, self.route))
        first = grid.c == 0
        x, y = grid.x, grid.y
        if self.stage == 0:
            total = total.reshape(2, grid.zs, 2, n, D)
            self.sent = jnp.where(first, take(total, 1 - x, 2), take(total, 1 - y, 0).swapaxes(0, 1))
            self.keep = jnp.where(first, take(total, x, 2), take(total, y, 0).swapaxes(0, 1))
            self.route = x_then_y
        elif self.stage == 1:
            at = jnp.where(first, y, x)
            self.sent, self.keep = take(total, 1 - at), take(total, at)
            self.route = y_then_x
        elif self.stage - 2 < len(self.bits):
            bit = self.bits[self.stage - 2]
            at = (grid.z // bit) % 2
            total = total.reshape(-1, 2, n, D)
            self.sent, self.keep = take(total, 1 - at, 1), take(total, at, 1)
            self.route = over_z(bit)
        else:
            return total[0]
        self.stage += 1
        return self.sent

    def hold(self, *others):
        self.keep = after(self.keep, *others)

    def left(self):
        return self.stage - 2 < len(self.bits)

    def finish(self):
        while self.left():
            self.step()
        return self.step()


def reduce_rows(grid, grads, n):
    view = grads.reshape(2, 2, grid.shards, n, D)
    return Reduction(grid, take(view, 1 - grid.c, 1), take(view, grid.c, 1))


def share_unit(grid, unit):
    pair = jnp.stack([unit, grid.move(unit, over_y)])
    both = jnp.stack([pair, grid.move(pair, over_core)], axis=1).reshape((4,) + unit.shape)
    return [take(both, jnp.bitwise_xor(grid.r, r)) for r in range(4)]


def norm_forward(values, scales, offset):
    center = values - jnp.mean(values, axis=-1, keepdims=True)
    inverse = lax.rsqrt(jnp.mean(center * center, axis=-1, keepdims=True) + norm_eps)
    norm_hat = center * inverse
    return (norm_hat * scales + offset, norm_hat, inverse)


def norm_backward(gradient, norm_hat, inverse, scales):
    hat_grad = gradient * scales
    value_grad = inverse * (
        hat_grad
        - jnp.mean(hat_grad, axis=-1, keepdims=True)
        - norm_hat * jnp.mean(hat_grad * norm_hat, axis=-1, keepdims=True)
    )
    return (value_grad, jnp.sum(gradient * norm_hat, axis=0), jnp.sum(gradient, axis=0))


def head_masks(rows):
    lane = lax.broadcasted_iota(jnp.int32, (rows, 128), 1)
    return (lane < HDIM, lane >= HDIM)


def dot_over(left, right, left_at, right_at):
    return lax.dot_general(
        left, right, (((left_at,), (right_at,)), ((), ())), preferred_element_type=f32
    )


def score_tile(keys, queries, tile, size):
    scores = dot_over(keys, queries, 1, 1)
    rows_at = lax.broadcasted_iota(jnp.int32, scores.shape, 0)
    cols_at = lax.broadcasted_iota(jnp.int32, scores.shape, 1) + tile * size
    return jnp.where(rows_at <= cols_at, scores, -1e30)


def attend_kernel(q_ref, k_ref, v_ref, c_ref, lse_ref):
    size = 256
    masks = head_masks(BLOCK)

    def slab(at, width, heads, first):
        columns = pl.ds(at, width)
        values = v_ref[:, columns]
        parts = []
        for h in range(heads):
            parts.append(jnp.where(masks[h], values, 0) if heads > 1 else values)
        for tile in range(BLOCK // size):
            extent = (tile + 1) * size
            keys = k_ref[pl.ds(0, extent), columns]
            queries = q_ref[pl.ds(tile * size, size), columns] * 0.125
            total = None
            for h in range(heads):
                mine = jnp.where(masks[h][:size], queries, 0) if heads > 1 else queries
                scores = score_tile(keys, mine, tile, size)
                top = jnp.max(scores, axis=0, keepdims=True)
                powers = jnp.exp(scores - top)
                norm = jnp.sum(powers, axis=0, keepdims=True)
                probs = (powers * (1.0 / norm)).astype(bf16)
                lse_ref[first + h, :, pl.ds(tile * size, size)] = top + jnp.log(norm)
                piece = dot_over(probs, parts[h][:extent], 0, 0)
                total = piece if total is None else total + piece
            c_ref[pl.ds(tile * size, size), columns] = total.astype(bf16)

    def pair(i, _):
        slab(pl.multiple_of(i * 128, 128), 128, 2, 2 * i)
        return 0

    lax.fori_loop(0, HEADS // 2, pair, 0)
    slab((HEADS - 1) * HDIM, HDIM, 1, HEADS - 1)


def attend_back_kernel(q_ref, k_ref, v_ref, lse_ref, dc_ref, dq_ref, dk_ref, dv_ref):
    size = 256
    masks = head_masks(BLOCK)

    def slab(at, width, heads, first):
        columns = pl.ds(at, width)
        keys_all = k_ref[:, columns]
        key_parts = [jnp.where(masks[h], keys_all, 0) if heads > 1 else keys_all for h in range(heads)]
        dk_total, dv_total = None, None
        for tile in reversed(range(BLOCK // size)):
            extent = (tile + 1) * size
            keys = keys_all[:extent]
            values = v_ref[pl.ds(0, extent), columns]
            queries = q_ref[pl.ds(tile * size, size), columns] * 0.125
            grads = dc_ref[pl.ds(tile * size, size), columns]
            dq_total, dk_tile, dv_tile = None, None, None
            for h in range(heads):
                my_q = jnp.where(masks[h][:size], queries, 0) if heads > 1 else queries
                my_g = jnp.where(masks[h][:size], grads, 0) if heads > 1 else grads
                scores = score_tile(keys, my_q, tile, size)
                probs = jnp.exp(scores - lse_ref[first + h, :, pl.ds(tile * size, size)])
                prob_grad = dot_over(values, my_g, 1, 1)
                inner = jnp.sum(probs * prob_grad, axis=0, keepdims=True)
                score_grad = (probs * (prob_grad - inner)).astype(bf16)
                dv = dot_over(probs.astype(bf16), my_g, 1, 0)
                dk = dot_over(score_grad, my_q, 1, 0)
                dq = dot_over(score_grad, key_parts[h][:extent], 0, 0)
                dv_tile = dv if dv_tile is None else dv_tile + dv
                dk_tile = dk if dk_tile is None else dk_tile + dk
                dq_total = dq if dq_total is None else dq_total + dq
            dq_ref[pl.ds(tile * size, size), columns] = (dq_total * 0.125).astype(bf16)
            if dk_total is None:
                dk_total, dv_total = dk_tile, dv_tile
            else:
                dk_total = jnp.concatenate([dk_total[:extent] + dk_tile, dk_total[extent:]])
                dv_total = jnp.concatenate([dv_total[:extent] + dv_tile, dv_total[extent:]])
        dk_ref[:, columns] = dk_total.astype(bf16)
        dv_ref[:, columns] = dv_total.astype(bf16)

    def pair(i, _):
        slab(pl.multiple_of(i * 128, 128), 128, 2, 2 * i)
        return 0

    lax.fori_loop(0, HEADS // 2, pair, 0)
    slab((HEADS - 1) * HDIM, HDIM, 1, HEADS - 1)


def part_block(part):
    return pl.BlockSpec((None, BLOCK, D), lambda i: (part, i, 0))


def attend(qkv, ties=()):
    rows = qkv.shape[1]
    block = pl.BlockSpec((BLOCK, D), lambda i: (i, 0))
    lse = pl.BlockSpec((HEADS, 1, BLOCK), lambda i: (0, 0, i))
    return call(
        attend_kernel,
        "attend",
        14_000_000_000,
        (qkv, qkv, qkv),
        ties,
        grid=(rows // BLOCK,),
        in_specs=[part_block(0), part_block(1), part_block(2)],
        out_specs=[block, lse],
        out_shape=[
            jax.ShapeDtypeStruct((rows, D), bf16),
            jax.ShapeDtypeStruct((HEADS, 1, rows), f32),
        ],
    )


def attend_back(qkv, lse, context_grad, ties=()):
    rows = qkv.shape[1]
    block = pl.BlockSpec((BLOCK, D), lambda i: (i, 0))
    lse_block = pl.BlockSpec((HEADS, 1, BLOCK), lambda i: (0, 0, i))
    return call(
        attend_back_kernel,
        "attend_back",
        18_000_000_000,
        (qkv, qkv, qkv, lse, context_grad),
        ties,
        grid=(rows // BLOCK,),
        in_specs=[part_block(0), part_block(1), part_block(2), lse_block, block],
        out_specs=[block] * 3,
        out_shape=[jax.ShapeDtypeStruct((rows, D), bf16)] * 3,
    )


def call(kernel, name, flops, operands, ties=(), in_specs=(), **kw):
    count = len(operands)

    def body(*refs):
        kernel(*refs[:count], *refs[count + len(ties) :])

    return pl.pallas_call(
        body,
        in_specs=list(in_specs) + [pl.BlockSpec(memory_space=pl.ANY)] * len(ties),
        compiler_params=pltpu.CompilerParams(vmem_limit_bytes=VMEM_LIMIT),
        cost_estimate=pl.CostEstimate(flops=flops, bytes_accessed=20_000_000, transcendentals=0),
        name=name,
        **kw,
    )(*operands, *ties)


def weight_grad_kernel(left_ref, right_ref, out_ref):
    out_ref[...] = dot_over(left_ref[...], right_ref[...], 0, 0).astype(bf16)


def weight_grad(left, right, ties=()):
    rows, wide = left.shape
    tile = 512
    return call(
        weight_grad_kernel,
        "weight_grad",
        2 * rows * wide * D,
        (left, right),
        ties,
        grid=(pl.cdiv(wide, tile),),
        in_specs=[
            pl.BlockSpec((rows, tile), lambda i: (0, i)),
            pl.BlockSpec((rows, D), lambda i: (0, 0)),
        ],
        out_specs=pl.BlockSpec((tile, D), lambda i: (i, 0)),
        out_shape=jax.ShapeDtypeStruct((wide, D), bf16),
    )


def up_kernel(second_ref, up_ref, bias_ref, active_ref, slope_ref):
    pre = dot_over(second_ref[...], up_ref[...], 1, 1) + bias_ref[...]
    root = math.sqrt(2.0 / math.pi)
    square = pre * pre
    curve = jnp.tanh(pre * (root + (root * 0.044715) * square))
    half = 0.5 + 0.5 * curve
    active_ref[...] = (pre * half).astype(bf16)
    inner = root + (3.0 * root * 0.044715) * square
    slope_ref[...] = (half + (0.5 * pre) * (1.0 - curve * curve) * inner).astype(bf16)


def up_forward(second, up_full, bias, ties=()):
    rows, ff = second.shape[0], up_full.shape[0]
    tile = 512
    columns = pl.BlockSpec((rows, tile), lambda i: (0, i))
    return call(
        up_kernel,
        "up_forward",
        2 * rows * ff * D,
        (second, up_full, bias.reshape(1, ff)),
        ties,
        grid=(pl.cdiv(ff, tile),),
        in_specs=[
            pl.BlockSpec((rows, D), lambda i: (0, 0)),
            pl.BlockSpec((tile, D), lambda i: (i, 0)),
            pl.BlockSpec((1, tile), lambda i: (0, i)),
        ],
        out_specs=[columns, columns],
        out_shape=[jax.ShapeDtypeStruct((rows, ff), bf16)] * 2,
    )


def active_back_kernel(grad_ref, down_ref, slope_ref, out_ref, sum_ref):
    active_grad = dot_over(grad_ref[...], down_ref[...], 1, 1)
    low = (active_grad * slope_ref[...].astype(f32)).astype(bf16)
    out_ref[...] = low
    sum_ref[...] = jnp.sum(low.astype(f32), axis=0, keepdims=True)


def active_back(grad_low, down_full, slope, ties=()):
    rows, ff = slope.shape
    tile = 512
    columns = pl.BlockSpec((rows, tile), lambda i: (0, i))
    return call(
        active_back_kernel,
        "active_back",
        2 * rows * ff * D,
        (grad_low, down_full, slope),
        ties,
        grid=(pl.cdiv(ff, tile),),
        in_specs=[
            pl.BlockSpec((rows, D), lambda i: (0, 0)),
            pl.BlockSpec((tile, D), lambda i: (i, 0)),
            columns,
        ],
        out_specs=[columns, pl.BlockSpec((1, tile), lambda i: (0, i))],
        out_shape=[
            jax.ShapeDtypeStruct((rows, ff), bf16),
            jax.ShapeDtypeStruct((1, ff), f32),
        ],
    )


def row_mean(value):
    return jnp.sum(value, axis=-1, keepdims=True) * (1.0 / D)


def norm_back_rows(base, gradient, scales):
    center = base - row_mean(base)
    inverse = lax.rsqrt(row_mean(center * center) + norm_eps)
    hat = center * inverse
    scaled = gradient * scales
    back = inverse * (scaled - row_mean(scaled) - hat * row_mean(scaled * hat))
    return back, gradient * hat


def up_back_kernel(up_low_ref, up_ref, residual_ref, grad_ref, scale_ref, out_ref, low_ref, sums_ref):
    second_grad = dot_over(up_low_ref[...], up_ref[...], 1, 0)
    back, with_hat = norm_back_rows(residual_ref[...], second_grad, scale_ref[...])
    total = grad_ref[...].astype(f32) + back
    low = total.astype(bf16)
    out_ref[...] = total
    low_ref[...] = low

    @pl.when(pl.program_id(0) == 0)
    def _():
        sums_ref[...] = jnp.zeros_like(sums_ref)

    for at, value in enumerate([with_hat, second_grad, low.astype(f32)]):
        sums_ref[pl.ds(at, 1), :] += jnp.sum(value, axis=0, keepdims=True)


def up_back(up_low, up_full, residual, grad_low, scale, ties=()):
    rows, ff = up_low.shape
    size = 256
    block = pl.BlockSpec((size, D), lambda i: (i, 0))
    return call(
        up_back_kernel,
        "up_back",
        2 * rows * ff * D,
        (up_low, up_full, residual, grad_low, scale.reshape(1, D)),
        ties,
        grid=(rows // size,),
        in_specs=[
            pl.BlockSpec((size, ff), lambda i: (i, 0)),
            pl.BlockSpec((ff, D), lambda i: (0, 0)),
            block,
            block,
            pl.BlockSpec((1, D), lambda i: (0, 0)),
        ],
        out_specs=[block, block, pl.BlockSpec((8, D), lambda i: (0, 0))],
        out_shape=[
            jax.ShapeDtypeStruct((rows, D), f32),
            jax.ShapeDtypeStruct((rows, D), bf16),
            jax.ShapeDtypeStruct((8, D), f32),
        ],
    )


def qkv_kernel(normed_ref, weight_ref, bias_ref, out_ref):
    out_ref[...] = (dot_over(normed_ref[...], weight_ref[...], 1, 0) + bias_ref[...]).astype(bf16)


def qkv_forward(normed, attn_full, bias_rows, ties=()):
    rows = normed.shape[0]
    return call(
        qkv_kernel,
        "qkv_forward",
        6 * rows * D * D,
        (normed, attn_full, bias_rows.reshape(3, 1, D)),
        ties,
        grid=(3,),
        in_specs=[
            pl.BlockSpec((rows, D), lambda i: (0, 0)),
            pl.BlockSpec((None, D, D), lambda i: (i, 0, 0)),
            pl.BlockSpec((None, 1, D), lambda i: (i, 0, 0)),
        ],
        out_specs=pl.BlockSpec((None, rows, D), lambda i: (i, 0, 0)),
        out_shape=jax.ShapeDtypeStruct((3, rows, D), bf16),
    )


def qkv_back_kernel(dq_ref, dk_ref, dv_ref, weight_ref, base_ref, resid_ref, scale_ref, out_ref, sums_ref):
    normed_grad = dot_over(dq_ref[...], weight_ref[0], 1, 1)
    normed_grad += dot_over(dk_ref[...], weight_ref[1], 1, 1)
    normed_grad += dot_over(dv_ref[...], weight_ref[2], 1, 1)
    back, with_hat = norm_back_rows(base_ref[...].astype(f32), normed_grad, scale_ref[...])
    out_ref[...] = resid_ref[...] + back

    @pl.when(pl.program_id(0) == 0)
    def _():
        sums_ref[...] = jnp.zeros_like(sums_ref)

    totals = [with_hat, normed_grad, dq_ref[...].astype(f32), dv_ref[...].astype(f32)]
    for at, value in enumerate(totals):
        sums_ref[pl.ds(at, 1), :] += jnp.sum(value, axis=0, keepdims=True)


def qkv_back(rows_grad, attn_full, base, resid_grad, scale, ties=()):
    rows = base.shape[0]
    size = 256
    block = pl.BlockSpec((size, D), lambda i: (i, 0))
    return call(
        qkv_back_kernel,
        "qkv_back",
        6 * rows * D * D,
        (*rows_grad, attn_full, base, resid_grad, scale.reshape(1, D)),
        ties,
        grid=(rows // size,),
        in_specs=[block] * 3
        + [
            pl.BlockSpec((3, D, D), lambda i: (0, 0, 0)),
            block,
            block,
            pl.BlockSpec((1, D), lambda i: (0, 0)),
        ],
        out_specs=[block, pl.BlockSpec((8, D), lambda i: (0, 0))],
        out_shape=[
            jax.ShapeDtypeStruct((rows, D), f32),
            jax.ShapeDtypeStruct((8, D), f32),
        ],
    )


def plain_add_kernel(first_ref, second_ref, out_ref):
    out_ref[...] = first_ref[...] + second_ref[...]


def plain_add(first, second, ties=()):
    whole = pl.BlockSpec(first.shape, lambda: (0, 0))
    return call(
        plain_add_kernel,
        "plain_add",
        first.size,
        (first, second),
        ties,
        in_specs=[whole, whole],
        out_specs=whole,
        out_shape=jax.ShapeDtypeStruct(first.shape, f32),
    )


def adam_update(weight, mean_old, square_old, gradient, step_rate, decay_rate):
    mean_new = beta_first * mean_old + (1.0 - beta_first) * gradient
    square_new = beta_second * square_old + (1.0 - beta_second) * gradient * gradient
    mean_hat = mean_new / (1.0 - beta_first**STEP)
    square_hat = square_new / (1.0 - beta_second**STEP)
    weight_new = weight - step_rate * (
        mean_hat / (jnp.sqrt(square_hat) + adam_floor) + decay_rate * weight
    )
    return (weight_new, mean_new, square_new)


def per_device(
    hidden_in,
    cotangent,
    lengths,
    qkv_weight,
    qkv_mean,
    qkv_square,
    out_weight,
    out_mean,
    out_square,
    up_weight,
    up_mean,
    up_square,
    down_weight,
    down_mean,
    down_square,
    vectors,
    vectors_mean,
    vectors_square,
    upbias,
    upbias_mean,
    upbias_square,
):
    shards = (qkv_weight, out_weight, up_weight, down_weight, vectors, upbias)
    first_moments = (qkv_mean, out_mean, up_mean, down_mean, vectors_mean, upbias_mean)
    squares = (qkv_square, out_square, up_square, down_square, vectors_square, upbias_square)
    grid = Grid()
    n = D // grid.shards
    slots = hidden_in.shape[0]
    row_count = slots * BLOCK
    ff = 4 * D

    attn_units = jnp.stack(
        [qkv_weight[:, :D], qkv_weight[:, D : 2 * D], qkv_weight[:, 2 * D :], out_weight]
    )
    attn_unit = take(attn_units, grid.r).astype(bf16)
    small = jnp.concatenate([vectors.reshape(-1), upbias]).astype(bf16)
    small = jnp.pad(small, (0, EXTRA * D - small.shape[0])).reshape(EXTRA, D)
    attn_unit = jnp.concatenate([attn_unit, small])
    up_unit = lax.dynamic_slice_in_dim(up_weight, grid.r * n, n, 1).astype(bf16).T
    down_unit = lax.dynamic_slice_in_dim(down_weight, grid.r * n, n, 0).astype(bf16)

    got, offs = gather_z(grid, attn_unit)
    attn_z = [part[:, :n] for part in got]
    small_z = jnp.concatenate([part[:, n:] for part in got])
    up_z = gather_z(grid, after(up_unit, got[1]))[0]
    attn_xy, attn_pieces = gather_rest(grid, attn_z)
    up_held = after(jnp.concatenate(up_z), *attn_xy)
    up_both = jnp.stack([up_held, grid.move(up_held, y_then_x)])
    up_late = grid.move(up_both, x_then_y)
    down_unit = after(down_unit, *attn_pieces)
    joined = [offs[0] + offs[1]]
    attn_full = assemble(grid, attn_pieces, offs, n)

    own = small_z.reshape(grid.zs, EXTRA * D)[:, : 12 * n]
    pair = jnp.stack([own, grid.move(own, over_x)])
    pair = jnp.stack([take(pair, grid.x), take(pair, 1 - grid.x)])
    where_off = jnp.array([joined[0].index(z) for z in range(grid.zs)])
    pair = pair[:, where_off[jnp.bitwise_xor(grid.z, jnp.arange(grid.zs))]]
    smalls = pair.transpose(1, 0, 2).reshape(grid.shards, 12 * n)
    vec_values = (
        smalls[:, : 8 * n].reshape(grid.shards, 8, n).transpose(1, 0, 2).reshape(8, D).astype(f32)
    )
    bias_full = (
        smalls[:, 8 * n :].reshape(grid.shards, 4, n).transpose(1, 0, 2).reshape(ff).astype(f32)
    )

    attn_full = attn_full.reshape(4, D, D)
    out_full = attn_full[3]

    flat_in = hidden_in.reshape(row_count, D).astype(f32)
    positions = jnp.arange(BLOCK, dtype=jnp.int32)
    row_valid = (positions[None, :] < lengths[:, None]).astype(f32).reshape(row_count, 1)
    normed_one, hat_one, inv_one = norm_forward(flat_in, vec_values[0], vec_values[1])
    normed_low = normed_one.astype(bf16)
    bias_rows = jnp.stack([vec_values[2], jnp.zeros((D,), f32), vec_values[3]])
    qkv_rows = qkv_forward(normed_low, attn_full, bias_rows, [down_unit])
    up_late = after(up_late, qkv_rows)
    down_held = down_unit[None]
    for bit in reversed(z_bits(grid.zs)[1:]):
        down_held = jnp.concatenate([down_held, after(grid.move(down_held, over_z(bit)), qkv_rows)])
    context_flat, logsum = attend(qkv_rows, [up_late, down_held])
    up_pieces = [up_both, up_late] + [
        after(grid.move(p, over_core), context_flat) for p in (up_both, up_late)
    ]
    down_last = after(grid.move(down_held, over_z(1)), context_flat)
    context_flat = after(context_flat, down_last)
    down_held = jnp.concatenate([down_held, down_last])
    up_full = assemble(grid, up_pieces, joined, n).reshape(ff, D)
    residual = (
        flat_in + jnp.dot(context_flat, out_full, preferred_element_type=f32) + vec_values[4]
    )
    second_low = norm_forward(residual, vec_values[5], vec_values[6])[0].astype(bf16)
    down_got = after(grid.move(down_held, y_then_x), up_full, second_low)
    down_both = jnp.stack([down_held, down_got])
    active_low, slope = up_forward(second_low, up_full, bias_full, [down_both])
    down_late = after(grid.move(down_both, x_then_y), active_low)
    grad_out = cotangent.reshape(row_count, D).astype(f32) * row_valid
    grad_low = grad_out.astype(bf16)
    down_bias_grad = jnp.sum(grad_out, axis=0)
    down_grad = weight_grad(active_low, grad_low, [down_late])
    down_pieces = [down_both, down_late] + [
        after(grid.move(p, over_core), down_grad) for p in (down_both, down_late)
    ]
    down_full = assemble(grid, down_pieces, joined, n).reshape(ff, D)
    down_sum = reduce_rows(grid, after(down_grad, *down_pieces), n)
    down_out = jnp.dot(active_low, down_full, preferred_element_type=f32) + vec_values[7]
    output = ((residual + down_out) * row_valid).astype(bf16).reshape(slots, BLOCK, D)

    up_low, upbias_grad = active_back(grad_low, down_full, slope, [down_sum.sent])
    down_sum.hold(up_low)
    down_sent = down_sum.step()
    up_sum = reduce_rows(grid, weight_grad(up_low, second_low, [down_sent]), n)
    resid_grad, branch_low, norm_sums = up_back(
        up_low, up_full, residual, grad_low, vec_values[5], [up_sum.sent]
    )
    scale_two_grad, offset_two_grad, out_bias_grad = norm_sums[0], norm_sums[1], norm_sums[2]
    for each in (down_sum, up_sum):
        each.hold(branch_low)
    down_sent, up_sent = down_sum.step(), up_sum.step()
    out_grad = jnp.einsum(
        "nd,ne->de", context_flat, branch_low, preferred_element_type=f32
    ).astype(bf16)
    context_grad = jnp.einsum("ne,de->nd", branch_low, out_full, preferred_element_type=f32)
    rows_grad = attend_back(
        qkv_rows, logsum, context_grad.astype(bf16), [down_sent, up_sent, out_grad]
    )
    for each in (down_sum, up_sum):
        each.hold(rows_grad[0])
    rows_grad = after(tuple(rows_grad), up_sum.step(), down_sum.step())
    query_grad, key_grad, value_grad = [
        jnp.einsum("nd,ne->de", normed_low, part, preferred_element_type=f32).astype(bf16)
        for part in rows_grad
    ]
    first = grid.c == 0
    theirs = jnp.stack([jnp.where(first, key_grad, query_grad), jnp.where(first, out_grad, value_grad)])
    mine = jnp.stack([jnp.where(first, query_grad, key_grad), jnp.where(first, value_grad, out_grad)])
    split = (2, grid.shards, n, D)
    attn_sum = Reduction(grid, theirs.reshape(split), mine.reshape(split))
    attn_sent = attn_sum.step()
    input_grad, first_sums = qkv_back(
        rows_grad,
        attn_full,
        hidden_in.reshape(row_count, D),
        resid_grad,
        vec_values[0],
        [attn_sent],
    )
    input_grad = input_grad.reshape(slots, BLOCK, D)
    small_grad = jnp.concatenate(
        [first_sums[:4], out_bias_grad[None], norm_sums[:2], down_bias_grad[None]]
        + [upbias_grad.reshape(4, D)]
    )
    attn_sum.hold(first_sums)
    waits = [output]
    routes = [over_core, over_y, over_x] + [over_z(bit) for bit in z_bits(grid.zs)]
    for route in routes:
        if attn_sum.left():
            attn_sent = attn_sum.step()
            for each in (up_sum, down_sum):
                if each.left():
                    each.hold(attn_sent)
                    each.step()
            if waits:
                attn_sum.hold(*waits)
            waits = []
        small_grad = plain_add(small_grad, grid.move(small_grad, route), [attn_sent])
    attn_unit_grad = attn_sum.finish()
    down_unit_grad = down_sum.finish()
    up_unit_grad = up_sum.finish()
    small_own = lax.dynamic_slice_in_dim(small_grad, (2 * grid.z + grid.x) * n, n, 1)

    down_parts = share_unit(grid, down_unit_grad)
    up_parts = share_unit(grid, up_unit_grad)
    attn_parts = share_unit(grid, attn_unit_grad)
    reduced = (
        jnp.concatenate(attn_parts[:3], axis=1).astype(f32),
        attn_parts[3].astype(f32),
        jnp.concatenate(up_parts).T.astype(f32),
        jnp.concatenate(down_parts).astype(f32),
        small_own[:8],
        small_own[8:].reshape(-1),
    )
    updates = []
    for group_index in range(6):
        updates.extend(
            adam_update(
                shards[group_index],
                first_moments[group_index],
                squares[group_index],
                reduced[group_index],
                step_rates[group_index],
                decay_rates[group_index],
            )
        )
    return (output, input_grad) + tuple(updates)


def solution(mesh):
    tokens = P(("fsdp", "dp"), None, None)
    rows, columns = P("fsdp", None), P(None, "fsdp")
    state = (rows,) * 6 + (columns,) * 3 + (rows,) * 3 + (columns,) * 3 + (P("fsdp"),) * 3
    return jax.shard_map(
        per_device,
        mesh=mesh,
        in_specs=(tokens, tokens, P(("fsdp", "dp"))) + state,
        out_specs=(tokens, tokens) + state,
        check_vma=False,
    )
```

profile of v0, /device:TPU:0, one launch (start us, length us, event | category | flops | bytes accessed | tf_op | source)
XLA Modules:
  0.0 596.5 jit_solution(7311326465073055804)
XLA Ops:
  10.1 13.3 %collective-permute-done = bf16[1,144,1088]{2,1,0:T(8,128)(2,1)S(1)} collective-permute-done((bf16[1,144,1088]{2,1,0:T(8,128)(2,1)S(1)}, bf16[1,144,1088]{2,1,0:T(8,128)(2,1)S(1)}, u32[]{:S(2)}, u32[]{:S(2)}) %collective-permute-start) | collective-permute-done | bytes 313376 | tf_op jit(solution)/shard_map/ppermute | solution.py:51
  30.3 10.4 %collective-permute-done.1 = bf16[2,144,1088]{2,1,0:T(8,128)(2,1)} collective-permute-done((bf16[2,144,1088]{2,1,0:T(8,128)(2,1)}, bf16[2,144,1088]{2,1,0:T(8,128)(2,1)}, u32[]{:S(2)}, u32[]{:S(2)}) %collective-permute-start.1) | collective-permute-done | bytes 626720 | tf_op jit(solution)/shard_map/ppermute | solution.py:51
  65.8 11.3 %collective-permute-done.12 = bf16[2,136,1088]{2,1,0:T(8,128)(2,1)S(1)} collective-permute-done((bf16[2,136,1088]{2,1,0:T(8,128)(2,1)S(1)}, bf16[2,136,1088]{2,1,0:T(8,128)(2,1)S(1)}, u32[]{:S(2)}, u32[]{:S(2)}) %collective-permute-start.12) | collective-permute-done | bytes 591904 | tf_op jit(solution)/shard_map/ppermute | solution.py:51
  89.7 8.7 %collective-permute-done.13 = bf16[4,136,1088]{2,1,0:T(8,128)(2,1)} collective-permute-done((bf16[4,136,1088]{2,1,0:T(8,128)(2,1)S(1)}, bf16[4,136,1088]{2,1,0:T(8,128)(2,1)}, u32[]{:S(2)}, u32[]{:S(2)}) %collective-permute-start.13) | collective-permute-done | bytes 1183776 | tf_op jit(solution)/shard_map/ppermute | solution.py:51
  112.1 7.8 %assemble.3 = bf16[4,8,136,1088]{3,2,1,0:T(8,128)(2,1)} custom-call(bf16[2,2,136,1088]{3,2,1,0:T(8,128)(2,1)} %copy-done.12, bf16[2,2,136,1088]{3,2,1,0:T(8,128)(2,1)} %copy-done.32, bf16[2,2,136,1088]{3,2,1,0:T(8,128)(2,1)} %copy-done.13, bf16[2,2,136,1088]{3,2,1,0:T(8,128)(2,1)} %copy-done.33, bf16[2,2,136,1088]{3,2,1,0:T(8,128)(2,1)} %collective-permute-done.7.refs_4_, ...), custom_call_target="tpu_custom_call" | custom-call | bytes 20000000 | tf_op jit(solution)/shard_map/assemble/pallas_call | solution.py:141
  119.9 14.4 %qkv_forward.1.refs_0_.refs_1_.refs_2_ = bf16[3,1024,1088]{2,1,0:T(8,128)(2,1)} custom-call(bf16[1024,1088]{1,0:T(8,128)(2,1)} %fusion.3.refs_0_, bf16[4,1088,1088]{2,1,0:T(8,128)(2,1)} %bitcast.247, f32[3,1,1088]{2,1,0:T(1,128)} %reshape.294.refs_2_, bf16[136,1088]{1,0:T(8,128)(2,1)} %dynamic-slice_convert_fusion.1.refs_3_), custom_call_target="tpu_custom_call" | custom-call | flops 7272923136 | bytes 20000000 | tf_op jit(solution)/shard_map/qkv_forward/pallas_call | solution.py:381
  138.2 23.1 %attend.1 = (bf16[1024,1088]{1,0:T(8,128)(2,1)}, f32[17,1,1024]{2,1,0:T(1,128)}) custom-call(bf16[3,1024,1088]{2,1,0:T(8,128)(2,1)} %qkv_forward.1.refs_0_.refs_1_.refs_2_, bf16[3,1024,1088]{2,1,0:T(8,128)(2,1)} %qkv_forward.1.refs_0_.refs_1_.refs_2_, bf16[3,1024,1088]{2,1,0:T(8,128)(2,1)} %qkv_forward.1.refs_0_.refs_1_.refs_2_, ...), custom_call_target="tpu_custom_call" | custom-call | flops 14000000000 | bytes 20000000 | tf_op jit(solution)/shard_map/attend/pallas_call | solution.py:381
  163.4 5.4 fusion.48
  171.8 7.4 %assemble.4 = bf16[4,8,136,1088]{3,2,1,0:T(8,128)(2,1)} custom-call(bf16[2,4,136,1088]{3,2,1,0:T(8,128)(2,1)} %copy-done.3, bf16[2,4,136,1088]{3,2,1,0:T(8,128)(2,1)} %collective-permute-done.14.refs_3_.refs_1_, bf16[2,4,136,1088]{3,2,1,0:T(8,128)(2,1)} %collective-permute-done.17.refs_2_, bf16[2,4,136,1088]{3,2,1,0:T(8,128)(2,1)} %collective-permute-done.18.refs_3_), custom_call_target="tpu_custom_call" | custom-call | bytes 20000000 | tf_op jit(solution)/shard_map/assemble/pallas_call | solution.py:141
  184.6 26.0 %up_forward.1 = (bf16[1024,4352]{1,0:T(8,128)(2,1)}, bf16[1024,4352]{1,0:T(8,128)(2,1)}) custom-call(bf16[1024,1088]{1,0:T(8,128)(2,1)} %add_convert_fusion.6.refs_0_.refs_1_, bf16[4352,1088]{1,0:T(8,128)(2,1)} %bitcast.255, f32[1,4352]{1,0:T(1,128)} %reshape.312.refs_2_, bf16[2,4,136,1088]{3,2,1,0:T(8,128)(2,1)} %copy-done.4), custom_call_target="tpu_custom_call" | custom-call | flops 9697230848 | bytes 20000000 | tf_op jit(solution)/shard_map/up_forward/pallas_call | solution.py:381
  221.7 17.3 %weight_grad.2 = bf16[4352,1088]{1,0:T(8,128)(2,1)} custom-call(bf16[1024,4352]{1,0:T(8,128)(2,1)} %get-tuple-element.72.refs_0_, bf16[1024,1088]{1,0:T(8,128)(2,1)} %fusion.5.refs_1_.refs_0_.refs_3_, bf16[2,4,136,1088]{3,2,1,0:T(8,128)(2,1)} %collective-permute-done.20.refs_2_.refs_1_), custom_call_target="tpu_custom_call" | custom-call | flops 9697230848 | bytes 20000000 | tf_op jit(solution)/shard_map/weight_grad/pallas_call | solution.py:381
  239.0 8.6 %dynamic-slice_bitcast_fusion.2 = (bf16[2,8,136,1088]{3,2,1,0:T(8,128)(2,1)}, bf16[2,8,136,1088]{3,2,1,0:T(8,128)(2,1)}) fusion(bf16[2,2,8,136,1088]{4,3,2,1,0:T(8,128)(2,1)} %bitcast.249, s32[]{:T(128)S(6)} %select_n.223, s32[]{:T(128)S(6)} %select_n.221), kind=kLoop, calls=%fused_computation.19 | loop fusion | bytes 18939912 | tf_op jit(solution)/shard_map/jit(dynamic_index_in_dim)/squeeze | solution.py:83
  248.1 7.4 %assemble.5 = bf16[4,8,136,1088]{3,2,1,0:T(8,128)(2,1)} custom-call(bf16[2,4,136,1088]{3,2,1,0:T(8,128)(2,1)} %copy-done.4, bf16[2,4,136,1088]{3,2,1,0:T(8,128)(2,1)} %collective-permute-done.20.refs_2_.refs_1_, bf16[2,4,136,1088]{3,2,1,0:T(8,128)(2,1)} %collective-permute-done.21.refs_2_, bf16[2,4,136,1088]{3,2,1,0:T(8,128)(2,1)} %collective-permute-done.22.refs_3_), custom_call_target="tpu_custom_call" | custom-call | bytes 20000000 | tf_op jit(solution)/shard_map/assemble/pallas_call | solution.py:141
  255.5 19.5 %active_back.1 = (bf16[1024,4352]{1,0:T(8,128)(2,1)}, f32[1,4352]{1,0:T(1,128)}) custom-call(bf16[1024,1088]{1,0:T(8,128)(2,1)} %fusion.5.refs_1_.refs_0_.refs_3_, bf16[4352,1088]{1,0:T(8,128)(2,1)} %bitcast.251, bf16[1024,4352]{1,0:T(8,128)(2,1)} %get-tuple-element.77.refs_2_, bf16[2,8,136,1088]{3,2,1,0:T(8,128)(2,1)} %get-tuple-element.231.refs_3_), custom_call_target="tpu_custom_call" | custom-call | flops 9697230848 | bytes 20000000 | tf_op jit(solution)/shard_map/active_back/pallas_call | solution.py:381
  281.2 17.3 %weight_grad.3 = bf16[4352,1088]{1,0:T(8,128)(2,1)} custom-call(bf16[1024,4352]{1,0:T(8,128)(2,1)} %get-tuple-element.79.refs_0_, bf16[1024,1088]{1,0:T(8,128)(2,1)} %add_convert_fusion.6.refs_0_.refs_1_, bf16[2,4,136,1088]{3,2,1,0:T(8,128)(2,1)} %get-tuple-element.245.refs_2_), custom_call_target="tpu_custom_call" | custom-call | flops 9697230848 | bytes 20000000 | tf_op jit(solution)/shard_map/weight_grad/pallas_call | solution.py:381
  298.5 8.6 %dynamic-slice_bitcast_fusion = (bf16[2,8,136,1088]{3,2,1,0:T(8,128)(2,1)}, bf16[2,8,136,1088]{3,2,1,0:T(8,128)(2,1)}) fusion(bf16[2,2,8,136,1088]{4,3,2,1,0:T(8,128)(2,1)} %bitcast.250, s32[]{:T(128)S(6)} %select_n.223, s32[]{:T(128)S(6)} %select_n.221), kind=kLoop, calls=%fused_computation.16 | loop fusion | bytes 18939912 | tf_op jit(solution)/shard_map/jit(dynamic_index_in_dim)/squeeze | solution.py:83
  308.8 21.5 %up_back.1 = (f32[1024,1088]{1,0:T(8,128)}, bf16[1024,1088]{1,0:T(8,128)(2,1)}, f32[8,1088]{1,0:T(8,128)}) custom-call(bf16[1024,4352]{1,0:T(8,128)(2,1)} %get-tuple-element.79.refs_0_, bf16[4352,1088]{1,0:T(8,128)(2,1)} %bitcast.256, f32[1024,1088]{1,0:T(8,128)} %copy-done.2, bf16[1024,1088]{1,0:T(8,128)(2,1)} %fusion.5.refs_1_.refs_0_.refs_3_, ...), custom_call_target="tpu_custom_call" | custom-call | flops 9697230848 | bytes 20000000 | tf_op jit(solution)/shard_map/up_back/pallas_call | solution.py:381
  330.3 6.0 convolution_convert_fusion.4
  340.8 7.1 %convolution_convert_fusion.3.refs_7_ = bf16[1088,1088]{1,0:T(8,128)(2,1)} fusion(bf16[1024,1088]{1,0:T(8,128)(2,1)} %get-tuple-element.68, bf16[1024,1088]{1,0:T(8,128)(2,1)} %get-tuple-element.81), kind=kOutput, calls=%fused_computation.8 | convolution fusion | flops 2425491456 | bytes 6823936 | tf_op jit(solution)/shard_map/nd,ne->de/dot_general | solution.py:747
  358.5 31.0 %attend_back.1 = (bf16[1024,1088]{1,0:T(8,128)(2,1)}, bf16[1024,1088]{1,0:T(8,128)(2,1)}, bf16[1024,1088]{1,0:T(8,128)(2,1)}) custom-call(bf16[3,1024,1088]{2,1,0:T(8,128)(2,1)} %qkv_forward.1.refs_0_.refs_1_.refs_2_, bf16[3,1024,1088]{2,1,0:T(8,128)(2,1)} %qkv_forward.1.refs_0_.refs_1_.refs_2_, bf16[3,1024,1088]{2,1,0:T(8,128)(2,1)} %qkv_forward.1.refs_0_.refs_1_.refs_2_, ...), custom_call_target="tpu_custom_call" | custom-call | flops 17999998976 | bytes 20000000 | tf_op jit(solution)/shard_map/attend_back/pallas_call | solution.py:381
  417.0 6.8 %collective-permute-done.28 = bf16[2,8,136,1088]{3,2,1,0:T(8,128)(2,1)} collective-permute-done((bf16[2,8,136,1088]{3,2,1,0:T(8,128)(2,1)}, bf16[2,8,136,1088]{3,2,1,0:T(8,128)(2,1)}, u32[]{:S(2)}, u32[]{:S(2)}) %collective-permute-start.28) | collective-permute-done | bytes 4735008 | tf_op jit(solution)/shard_map/ppermute | solution.py:51
  423.8 5.4 add_convert_fusion
  432.2 6.4 %bitcast_select_fusion.4 = (bf16[2,4,136,1088]{3,2,1,0:T(8,128)(2,1)}, bf16[2,4,136,1088]{3,2,1,0:T(8,128)(2,1)}) fusion(bf16[1,4,2,136,1088]{4,3,2,1,0:T(8,128)(2,1)} %get-tuple-element.234, bf16[2,4,2,136,1088]{4,3,2,1,0:T(8,128)(2,1)S(1)} %bitcast.236, s32[]{:T(128)S(6)} %select_n.214, pred[]{:T(512)S(6)} %eq.18, ...), kind=kLoop, calls=%fused_computation.56 | loop fusion | flops 2367488 | bytes 14204937 | tf_op jit(solution)/shard_map/jit(_where)/select_n | solution.py:177
  439.7 15.4 %multiply_convert_fusion = bf16[1024,1088]{1,0:T(8,128)(2,1)} fusion(f32[1024,1088]{1,0:T(8,128)S(1)} %bitcast.246, bf16[1024,4352]{1,0:T(8,128)(2,1)} %get-tuple-element.72.refs_0_, bf16[4352,1088]{1,0:T(8,128)(2,1)S(1)} %bitcast.254, f32[1088]{0:T(1024)S(1)} %add.366, f32[1024]{0:T(1024)S(1)} %bitcast.295), kind=kOutput, calls=%fused_computation.28 | convolution fusion | flops 9701687296 | bytes 25075968 | tf_op jit(solution)/shard_map/dot_general | solution.py:733
  458.3 19.6 %qkv_back.1 = (f32[1024,1088]{1,0:T(8,128)}, f32[8,1088]{1,0:T(8,128)}) custom-call(bf16[1024,1088]{1,0:T(8,128)(2,1)} %get-tuple-element.89.refs_0_, bf16[1024,1088]{1,0:T(8,128)(2,1)} %get-tuple-element.90.refs_1_, bf16[1024,1088]{1,0:T(8,128)(2,1)} %get-tuple-element.91.refs_2_, bf16[4,1088,1088]{2,1,0:T(8,128)(2,1)} %bitcast.248, ...), custom_call_target="tpu_custom_call" | custom-call | flops 7272923136 | bytes 20000000 | tf_op jit(solution)/shard_map/qkv_back/pallas_call | solution.py:381
  487.2 14.1 %collective-permute-done.41 = bf16[1,136,1088]{2,1,0:T(8,128)(2,1)S(1)} collective-permute-done((bf16[1,136,1088]{2,1,0:T(8,128)(2,1)S(1)}, bf16[1,136,1088]{2,1,0:T(8,128)(2,1)S(1)}, u32[]{:S(2)}, u32[]{:S(2)}) %collective-permute-start.41) | collective-permute-done | bytes 295968 | tf_op jit(solution)/shard_map/ppermute | solution.py:51
  514.6 6.2 %copy.167 = f32[2,512,1088]{1,2,0:T(8,128)} copy(f32[2,512,1088]{2,1,0:T(8,128)} %bitcast.268) | data formatting | bytes 8912896
  531.5 7.6 %collective-permute-done.31 = bf16[2,136,1088]{2,1,0:T(8,128)(2,1)S(1)} collective-permute-done((bf16[2,136,1088]{2,1,0:T(8,128)(2,1)S(1)}, bf16[2,136,1088]{2,1,0:T(8,128)(2,1)S(1)}, u32[]{:S(2)}, u32[]{:S(2)}) %collective-permute-start.31) | collective-permute-done | bytes 591904 | tf_op jit(solution)/shard_map/ppermute | solution.py:51
  565.5 5.5 collective-permute-done.33
  575.2 5.4 multiply_subtract_fusion.1
  580.6 5.4 multiply_subtract_fusion
  590.7 5.4 multiply_subtract_fusion.2
  (371 shorter events, 219.1 us)
Async XLA Ops:
  4.4 19.0 %collective-permute-start = (bf16[1,144,1088]{2,1,0:T(8,128)(2,1)S(1)}, bf16[1,144,1088]{2,1,0:T(8,128)(2,1)S(1)}, u32[]{:S(2)}, u32[]{:S(2)}) collective-permute-start(bf16[1,144,1088]{2,1,0:T(8,128)(2,1)S(1)} %maximum_bitcast_fusion), channel_id=1, source_target_pairs={{0,16},{1,17},{2,18},{3,19},{4,20},{5,21},{6,22},{7,23},{8,24},{9,... | collective-permute-start | bytes 940040 | tf_op jit(solution)/shard_map/ppermute | solution.py:51
  27.8 21.8 %collective-permute-start.3 = (bf16[2,136,1088]{2,1,0:T(8,128)(2,1)}, bf16[2,136,1088]{2,1,0:T(8,128)(2,1)}, u32[]{:S(2)}, u32[]{:S(2)}) collective-permute-start(bf16[2,136,1088]{2,1,0:T(8,128)(2,1)} %fusion.15), channel_id=1, source_target_pairs={{0,2},{1,5},{2,0},{3,7},{4,6},{5,1},{6,4},{7,3},{8,10},{9,13},{10,... | collective-permute-start | bytes 1775624 | tf_op jit(solution)/shard_map/ppermute | solution.py:51
  50.8 27.5 %collective-permute-start.4 = (bf16[2,2,136,1088]{3,2,1,0:T(8,128)(2,1)S(1)}, bf16[2,2,136,1088]{3,2,1,0:T(8,128)(2,1)S(1)}, u32[]{:S(2)}, u32[]{:S(2)}) collective-permute-start(bf16[2,2,136,1088]{3,2,1,0:T(8,128)(2,1)S(1)} %pad_maximum_fusion.3.refs_0_), channel_id=1, source_target_pairs={{0,4},{1,3},{2,6},{3,1},{4,0},{5,7},{6,2},{7,5},{8,12},{9,11},{10,... | collective-permute-start | bytes 3551240 | tf_op jit(solution)/shard_map/ppermute | solution.py:51
  58.7 22.6 %collective-permute-start.6 = (bf16[2,2,136,1088]{3,2,1,0:T(8,128)(2,1)S(1)}, bf16[2,2,136,1088]{3,2,1,0:T(8,128)(2,1)S(1)}, u32[]{:S(2)}, u32[]{:S(2)}) collective-permute-start(bf16[2,2,136,1088]{3,2,1,0:T(8,128)(2,1)S(1)} %pad_maximum_fusion.4.refs_2_), channel_id=1, source_target_pairs={{0,4},{1,3},{2,6},{3,1},{4,0},{5,7},{6,2},{7,5},{8,12},{9,11},{10,... | collective-permute-start | bytes 3551240 | tf_op jit(solution)/shard_map/ppermute | solution.py:51
  81.3 17.1 %collective-permute-start.13 = (bf16[4,136,1088]{2,1,0:T(8,128)(2,1)S(1)}, bf16[4,136,1088]{2,1,0:T(8,128)(2,1)}, u32[]{:S(2)}, u32[]{:S(2)}) collective-permute-start(bf16[4,136,1088]{2,1,0:T(8,128)(2,1)S(1)} %pad_maximum_fusion.5), channel_id=1, source_target_pairs={{0,2},{1,5},{2,0},{3,7},{4,6},{5,1},{6,4},{7,3},{8,10},{9,13},{10,... | collective-permute-start | bytes 3551240 | tf_op jit(solution)/shard_map/ppermute | solution.py:51
  88.6 20.8 %collective-permute-start.7 = (bf16[2,2,136,1088]{3,2,1,0:T(8,128)(2,1)}, bf16[2,2,136,1088]{3,2,1,0:T(8,128)(2,1)}, u32[]{:S(2)}, u32[]{:S(2)}) collective-permute-start(bf16[2,2,136,1088]{3,2,1,0:T(8,128)(2,1)} %copy-done.12), channel_id=1, source_target_pairs={{0,1},{1,0},{2,3},{3,2},{4,5},{5,4},{6,7},{7,6},{8,9},{9,8},{10,11... | collective-permute-start | bytes 3551240 | tf_op jit(solution)/shard_map/ppermute | solution.py:51
  100.4 37.8 %collective-permute-start.14 = (bf16[2,4,136,1088]{3,2,1,0:T(8,128)(2,1)S(1)}, bf16[2,4,136,1088]{3,2,1,0:T(8,128)(2,1)}, u32[]{:S(2)}, u32[]{:S(2)}) collective-permute-start(bf16[2,4,136,1088]{3,2,1,0:T(8,128)(2,1)S(1)} %pad_maximum_fusion.1.refs_0_), channel_id=1, source_target_pairs={{0,4},{1,3},{2,6},{3,1},{4,0},{5,7},{6,2},{7,5},{8,12},{9,11},{10,... | collective-permute-start | bytes 7102472 | tf_op jit(solution)/shard_map/ppermute | solution.py:51
  109.5 53.1 %collective-permute-start.17 = (bf16[2,4,136,1088]{3,2,1,0:T(8,128)(2,1)S(1)}, bf16[2,4,136,1088]{3,2,1,0:T(8,128)(2,1)}, u32[]{:S(2)}, u32[]{:S(2)}) collective-permute-start(bf16[2,4,136,1088]{3,2,1,0:T(8,128)(2,1)S(1)} %pad_maximum_fusion.1.refs_0_), channel_id=1, source_target_pairs={{0,1},{1,0},{2,3},{3,2},{4,5},{5,4},{6,7},{7,6},{8,9},{9,8},{10,11... | collective-permute-start | bytes 7102472 | tf_op jit(solution)/shard_map/ppermute | solution.py:51
  109.6 26.7 %collective-permute-start.15 = (bf16[1,136,1088]{2,1,0:T(8,128)(2,1)S(1)}, bf16[1,136,1088]{2,1,0:T(8,128)(2,1)S(1)}, u32[]{:S(2)}, u32[]{:S(2)}) collective-permute-start(bf16[1,136,1088]{2,1,0:T(8,128)(2,1)S(1)} %bitcast.269), channel_id=1, source_target_pairs={{0,16},{1,17},{2,18},{3,19},{4,20},{5,21},{6,22},{7,23},{8,24},{9,... | collective-permute-start | bytes 887816 | tf_op jit(solution)/shard_map/ppermute | solution.py:51
  136.4 25.0 %collective-permute-start.16 = (bf16[2,136,1088]{2,1,0:T(8,128)(2,1)S(1)}, bf16[2,136,1088]{2,1,0:T(8,128)(2,1)S(1)}, u32[]{:S(2)}, u32[]{:S(2)}) collective-permute-start(bf16[2,136,1088]{2,1,0:T(8,128)(2,1)S(1)} %pad_maximum_fusion.14.refs_4_), channel_id=1, source_target_pairs={{0,8},{1,9},{2,10},{3,11},{4,12},{5,13},{6,14},{7,15},{8,0},{9,1},... | collective-permute-start | bytes 1775624 | tf_op jit(solution)/shard_map/ppermute | solution.py:51
  162.6 17.2 %collective-permute-start.19 = (bf16[4,136,1088]{2,1,0:T(8,128)(2,1)}, bf16[4,136,1088]{2,1,0:T(8,128)(2,1)S(1)}, u32[]{:S(2)}, u32[]{:S(2)}) collective-permute-start(bf16[4,136,1088]{2,1,0:T(8,128)(2,1)} %get-tuple-element.273), channel_id=1, source_target_pairs={{0,2},{1,5},{2,0},{3,7},{4,6},{5,1},{6,4},{7,3},{8,10},{9,13},{10,... | collective-permute-start | bytes 3551240 | tf_op jit(solution)/shard_map/ppermute | solution.py:51
  182.5 30.6 %collective-permute-start.20 = (bf16[2,4,136,1088]{3,2,1,0:T(8,128)(2,1)S(1)}, bf16[2,4,136,1088]{3,2,1,0:T(8,128)(2,1)}, u32[]{:S(2)}, u32[]{:S(2)}) collective-permute-start(bf16[2,4,136,1088]{3,2,1,0:T(8,128)(2,1)S(1)} %pad_maximum_fusion.2.refs_3_.refs_0_), channel_id=1, source_target_pairs={{0,4},{1,3},{2,6},{3,1},{4,0},{5,7},{6,2},{7,5},{8,12},{9,11},{10,... | collective-permute-start | bytes 7102472 | tf_op jit(solution)/shard_map/ppermute | solution.py:51
  184.6 54.4 %collective-permute-start.21 = (bf16[2,4,136,1088]{3,2,1,0:T(8,128)(2,1)S(1)}, bf16[2,4,136,1088]{3,2,1,0:T(8,128)(2,1)}, u32[]{:S(2)}, u32[]{:S(2)}) collective-permute-start(bf16[2,4,136,1088]{3,2,1,0:T(8,128)(2,1)S(1)} %pad_maximum_fusion.2.refs_3_.refs_0_), channel_id=1, source_target_pairs={{0,1},{1,0},{2,3},{3,2},{4,5},{5,4},{6,7},{7,6},{8,9},{9,8},{10,11... | collective-permute-start | bytes 7102472 | tf_op jit(solution)/shard_map/ppermute | solution.py:51
  213.1 25.9 %collective-permute-start.22 = (bf16[2,4,136,1088]{3,2,1,0:T(8,128)(2,1)}, bf16[2,4,136,1088]{3,2,1,0:T(8,128)(2,1)}, u32[]{:S(2)}, u32[]{:S(2)}) collective-permute-start(bf16[2,4,136,1088]{3,2,1,0:T(8,128)(2,1)} %collective-permute-done.20.refs_2_.refs_1_), channel_id=1, source_target_pairs={{0,1},{1,0},{2,3},{3,2},{4,5},{5,4},{6,7},{7,6},{8,9},{9,8},{10,11... | collective-permute-start | bytes 7102472 | tf_op jit(solution)/shard_map/ppermute | solution.py:51
  247.6 27.5 %collective-permute-start.23 = (bf16[2,8,136,1088]{3,2,1,0:T(8,128)(2,1)}, bf16[2,8,136,1088]{3,2,1,0:T(8,128)(2,1)}, u32[]{:S(2)}, u32[]{:S(2)}) collective-permute-start(bf16[2,8,136,1088]{3,2,1,0:T(8,128)(2,1)} %get-tuple-element.231.refs_3_), channel_id=1, source_target_pairs={{0,1},{1,0},{2,3},{3,2},{4,5},{5,4},{6,7},{7,6},{8,9},{9,8},{10,11... | collective-permute-start | bytes 14204936 | tf_op jit(solution)/shard_map/ppermute | solution.py:51
  307.1 44.1 %collective-permute-start.25 = (bf16[2,8,136,1088]{3,2,1,0:T(8,128)(2,1)}, bf16[2,8,136,1088]{3,2,1,0:T(8,128)(2,1)}, u32[]{:S(2)}, u32[]{:S(2)}) collective-permute-start(bf16[2,8,136,1088]{3,2,1,0:T(8,128)(2,1)} %get-tuple-element.229.refs_5_), channel_id=1, source_target_pairs={{0,1},{1,0},{2,3},{3,2},{4,5},{5,4},{6,7},{7,6},{8,9},{9,8},{10,11... | collective-permute-start | bytes 14204936 | tf_op jit(solution)/shard_map/ppermute | solution.py:51
  307.1 40.7 %collective-permute-start.24 = (bf16[2,4,136,1088]{3,2,1,0:T(8,128)(2,1)}, bf16[2,4,136,1088]{3,2,1,0:T(8,128)(2,1)}, u32[]{:S(2)}, u32[]{:S(2)}) collective-permute-start(bf16[2,4,136,1088]{3,2,1,0:T(8,128)(2,1)} %get-tuple-element.245.refs_2_), channel_id=1, source_target_pairs={{0,4},{1,3},{2,6},{3,1},{4,0},{5,7},{6,2},{7,5},{8,12},{9,11},{10,... | collective-permute-start | bytes 7102472 | tf_op jit(solution)/shard_map/ppermute | solution.py:51
  350.4 39.0 %collective-permute-start.27 = (bf16[4,136,1088]{2,1,0:T(8,128)(2,1)S(1)}, bf16[4,136,1088]{2,1,0:T(8,128)(2,1)}, u32[]{:S(2)}, u32[]{:S(2)}) collective-permute-start(bf16[4,136,1088]{2,1,0:T(8,128)(2,1)S(1)} %get-tuple-element.253.refs_5_), channel_id=1, source_target_pairs={{0,2},{1,5},{2,0},{3,7},{4,6},{5,1},{6,4},{7,3},{8,10},{9,13},{10,... | collective-permute-start | bytes 3551240 | tf_op jit(solution)/shard_map/ppermute | solution.py:51
  357.6 35.9 %collective-permute-start.26 = (bf16[2,4,136,1088]{3,2,1,0:T(8,128)(2,1)}, bf16[2,4,136,1088]{3,2,1,0:T(8,128)(2,1)}, u32[]{:S(2)}, u32[]{:S(2)}) collective-permute-start(bf16[2,4,136,1088]{3,2,1,0:T(8,128)(2,1)} %get-tuple-element.241.refs_6_), channel_id=1, source_target_pairs={{0,4},{1,3},{2,6},{3,1},{4,0},{5,7},{6,2},{7,5},{8,12},{9,11},{10,... | collective-permute-start | bytes 7102472 | tf_op jit(solution)/shard_map/ppermute | solution.py:51
  438.6 40.6 %collective-permute-start.29 = (bf16[2,4,136,1088]{3,2,1,0:T(8,128)(2,1)}, bf16[2,4,136,1088]{3,2,1,0:T(8,128)(2,1)}, u32[]{:S(2)}, u32[]{:S(2)}) collective-permute-start(bf16[2,4,136,1088]{3,2,1,0:T(8,128)(2,1)} %get-tuple-element.233.refs_7_), channel_id=1, source_target_pairs={{0,4},{1,3},{2,6},{3,1},{4,0},{5,7},{6,2},{7,5},{8,12},{9,11},{10,... | collective-permute-start | bytes 7102472 | tf_op jit(solution)/shard_map/ppermute | solution.py:51
  456.6 26.3 %collective-permute-start.40 = (bf16[2,136,1088]{2,1,0:T(8,128)(2,1)}, bf16[2,136,1088]{2,1,0:T(8,128)(2,1)}, u32[]{:S(2)}, u32[]{:S(2)}) collective-permute-start(bf16[2,136,1088]{2,1,0:T(8,128)(2,1)} %get-tuple-element.262), channel_id=1, source_target_pairs={{0,8},{1,9},{2,10},{3,11},{4,12},{5,13},{6,14},{7,15},{8,0},{9,1},... | collective-permute-start | bytes 1775624 | tf_op jit(solution)/shard_map/ppermute | solution.py:51
  457.6 26.8 %collective-permute-start.35 = (bf16[4,136,1088]{2,1,0:T(8,128)(2,1)}, bf16[4,136,1088]{2,1,0:T(8,128)(2,1)}, u32[]{:S(2)}, u32[]{:S(2)}) collective-permute-start(bf16[4,136,1088]{2,1,0:T(8,128)(2,1)} %get-tuple-element.249), channel_id=1, source_target_pairs={{0,2},{1,5},{2,0},{3,7},{4,6},{5,1},{6,4},{7,3},{8,10},{9,13},{10,... | collective-permute-start | bytes 3551240 | tf_op jit(solution)/shard_map/ppermute | solution.py:51
  478.8 42.0 %collective-permute-start.44 = (f32[12,1088]{1,0:T(8,128)S(1)}, f32[12,1088]{1,0:T(8,128)}, u32[]{:S(2)}, u32[]{:S(2)}) collective-permute-start(f32[12,1088]{1,0:T(8,128)S(1)} %concatenate.52.refs_0_), channel_id=1, source_target_pairs={{0,1},{1,0},{2,3},{3,2},{4,5},{5,4},{6,7},{7,6},{8,9},{9,8},{10,11... | collective-permute-start | bytes 156680 | tf_op jit(solution)/shard_map/ppermute | solution.py:51
  481.7 21.0 %collective-permute-start.30 = (bf16[4,136,1088]{2,1,0:T(8,128)(2,1)S(1)}, bf16[4,136,1088]{2,1,0:T(8,128)(2,1)S(1)}, u32[]{:S(2)}, u32[]{:S(2)}) collective-permute-start(bf16[4,136,1088]{2,1,0:T(8,128)(2,1)S(1)} %get-tuple-element.251.refs_2_), channel_id=1, source_target_pairs={{0,2},{1,5},{2,0},{3,7},{4,6},{5,1},{6,4},{7,3},{8,10},{9,13},{10,... | collective-permute-start | bytes 3551240 | tf_op jit(solution)/shard_map/ppermute | solution.py:51
  484.1 17.2 %collective-permute-start.41 = (bf16[1,136,1088]{2,1,0:T(8,128)(2,1)S(1)}, bf16[1,136,1088]{2,1,0:T(8,128)(2,1)S(1)}, u32[]{:S(2)}, u32[]{:S(2)}) collective-permute-start(bf16[1,136,1088]{2,1,0:T(8,128)(2,1)S(1)} %constant_dynamic-slice_fusion.1), channel_id=1, source_target_pairs={{0,16},{1,17},{2,18},{3,19},{4,20},{5,21},{6,22},{7,23},{8,24},{9,... | collective-permute-start | bytes 887816 | tf_op jit(solution)/shard_map/ppermute | solution.py:51
  486.2 22.1 %collective-permute-start.36 = (bf16[2,136,1088]{2,1,0:T(8,128)(2,1)S(1)}, bf16[2,136,1088]{2,1,0:T(8,128)(2,1)S(1)}, u32[]{:S(2)}, u32[]{:S(2)}) collective-permute-start(bf16[2,136,1088]{2,1,0:T(8,128)(2,1)S(1)} %get-tuple-element.268), channel_id=1, source_target_pairs={{0,8},{1,9},{2,10},{3,11},{4,12},{5,13},{6,14},{7,15},{8,0},{9,1},... | collective-permute-start | bytes 1775624 | tf_op jit(solution)/shard_map/ppermute | solution.py:51
  501.4 24.7 %collective-permute-start.42 = (bf16[136,1088]{1,0:T(8,128)(2,1)S(1)}, bf16[136,1088]{1,0:T(8,128)(2,1)S(1)}, u32[]{:S(2)}, u32[]{:S(2)}) collective-permute-start(bf16[136,1088]{1,0:T(8,128)(2,1)S(1)} %bitcast.283), channel_id=1, source_target_pairs={{0,2},{1,3},{2,0},{3,1},{4,6},{5,7},{6,4},{7,5},{8,10},{9,11},{10,... | collective-permute-start | bytes 887816 | tf_op jit(solution)/shard_map/ppermute | solution.py:51
  509.2 21.0 %collective-permute-start.37 = (bf16[1,136,1088]{2,1,0:T(8,128)(2,1)}, bf16[1,136,1088]{2,1,0:T(8,128)(2,1)S(1)}, u32[]{:S(2)}, u32[]{:S(2)}) collective-permute-start(bf16[1,136,1088]{2,1,0:T(8,128)(2,1)} %constant_dynamic-slice_fusion.2), channel_id=1, source_target_pairs={{0,16},{1,17},{2,18},{3,19},{4,20},{5,21},{6,22},{7,23},{8,24},{9,... | collective-permute-start | bytes 887816 | tf_op jit(solution)/shard_map/ppermute | solution.py:51
  526.2 17.8 %collective-permute-start.43 = (bf16[2,136,1088]{2,1,0:T(8,128)(2,1)S(1)}, bf16[2,136,1088]{2,1,0:T(8,128)(2,1)S(1)}, u32[]{:S(2)}, u32[]{:S(2)}) collective-permute-start(bf16[2,136,1088]{2,1,0:T(8,128)(2,1)S(1)} %get-tuple-element.277), channel_id=1, source_target_pairs={{0,1},{1,0},{2,3},{3,2},{4,5},{5,4},{6,7},{7,6},{8,9},{9,8},{10,11... | collective-permute-start | bytes 1775624 | tf_op jit(solution)/shard_map/ppermute | solution.py:51
  530.3 22.8 %collective-permute-start.38 = (bf16[136,1088]{1,0:T(8,128)(2,1)S(1)}, bf16[136,1088]{1,0:T(8,128)(2,1)S(1)}, u32[]{:S(2)}, u32[]{:S(2)}) collective-permute-start(bf16[136,1088]{1,0:T(8,128)(2,1)S(1)} %bitcast.284), channel_id=1, source_target_pairs={{0,2},{1,3},{2,0},{3,1},{4,6},{5,7},{6,4},{7,5},{8,10},{9,11},{10,... | collective-permute-start | bytes 887816 | tf_op jit(solution)/shard_map/ppermute | solution.py:51
  539.4 21.3 %collective-permute-start.32 = (bf16[1,136,1088]{2,1,0:T(8,128)(2,1)S(1)}, bf16[1,136,1088]{2,1,0:T(8,128)(2,1)}, u32[]{:S(2)}, u32[]{:S(2)}) collective-permute-start(bf16[1,136,1088]{2,1,0:T(8,128)(2,1)S(1)} %constant_dynamic-slice_fusion.3.refs_2_), channel_id=1, source_target_pairs={{0,16},{1,17},{2,18},{3,19},{4,20},{5,21},{6,22},{7,23},{8,24},{9,... | collective-permute-start | bytes 887816 | tf_op jit(solution)/shard_map/ppermute | solution.py:51
  553.2 18.1 %collective-permute-start.39 = (bf16[2,136,1088]{2,1,0:T(8,128)(2,1)S(1)}, bf16[2,136,1088]{2,1,0:T(8,128)(2,1)}, u32[]{:S(2)}, u32[]{:S(2)}) collective-permute-start(bf16[2,136,1088]{2,1,0:T(8,128)(2,1)S(1)} %get-tuple-element.279), channel_id=1, source_target_pairs={{0,1},{1,0},{2,3},{3,2},{4,5},{5,4},{6,7},{7,6},{8,9},{9,8},{10,11... | collective-permute-start | bytes 1775624 | tf_op jit(solution)/shard_map/ppermute | solution.py:51
  (87 other events, 777.7 us)
where the time goes:
time: 608 us; the launch traced here: 597 us
  Pallas kernels  220 us (36%)
  waiting for transfers between devices  105 us (17%)
  other arithmetic  89.2 us (15%)
  local copies, waits for them, and re-layouts  78.3 us (13%)
  starting transfers between devices  55.5 us (9%)
  matrix products  46.4 us (8%)
    pallas_call x14, Pallas kernels, call(): pl.pallas_call(body, in_specs=list(in_specs) + [pl.BlockSpec(memory_space...  197 us
    ppermute x49, waiting for transfers between devices, move(): return lax.ppermute(value, AXES, pairs)  105 us
    ppermute x49, starting transfers between devices, move(): return lax.ppermute(value, AXES, pairs)  55.5 us
    convert_element_type x15, other arithmetic, add(): return (first.astype(f32) + second.astype(f32)).astype(bf16)  26.1 us
    pallas_call x3, Pallas kernels, assemble(): pl.pallas_call(functools.partial(assemble_kernel, grid.zs, offs), out_sha...  22.6 us
    squeeze x13, local copies, waits for them, and re-layouts, take(): return lax.dynamic_index_in_dim(value, at, axis, keepdims=False)  22.3 us
    unnamed x146, local copies, waits for them, and re-layouts  21.7 us
    sub x6, other arithmetic, adam_update(): weight - step_rate * (mean_hat / (jnp.sqrt(square_hat) + adam_floor) + de...  19.8 us
  transfers between devices with their start and end apart: 49, of which 18 were waited for; matrix products, arithmetic and copies ran while one was open for 22% of the time, Pallas kernels for 34%

commit v1 on v0

--- a/solution.py
+++ b/solution.py
@@ -168,26 +168,34 @@
 
     def step(self):
         grid, n = self.grid, self.n
-        total = add(self.keep, grid.move(self.sent, self.route))
+        mine, got = self.keep, grid.move(self.sent, self.route)
         first = grid.c == 0
         x, y = grid.x, grid.y
         if self.stage == 0:
-            total = total.reshape(2, grid.zs, 2, n, D)
-            self.sent = jnp.where(first, take(total, 1 - x, 2), take(total, 1 - y, 0).swapaxes(0, 1))
-            self.keep = jnp.where(first, take(total, x, 2), take(total, y, 0).swapaxes(0, 1))
+            shape = (2, grid.zs, 2, n, D)
+
+            def pick(value, at_x, at_y):
+                value = value.reshape(shape)
+                return jnp.where(first, take(value, at_x, 2), take(value, at_y, 0).swapaxes(0, 1))
+
+            self.sent = add(pick(mine, 1 - x, 1 - y), pick(got, 1 - x, 1 - y))
+            mine, got = after(mine, self.sent), after(got, self.sent)
+            self.keep = add(pick(mine, x, y), pick(got, x, y))
             self.route = x_then_y
         elif self.stage == 1:
             at = jnp.where(first, y, x)
-            self.sent, self.keep = take(total, 1 - at), take(total, at)
+            self.sent = add(take(mine, 1 - at), take(got, 1 - at))
+            self.keep = add(take(mine, at), take(got, at))
             self.route = y_then_x
         elif self.stage - 2 < len(self.bits):
             bit = self.bits[self.stage - 2]
             at = (grid.z // bit) % 2
-            total = total.reshape(-1, 2, n, D)
-            self.sent, self.keep = take(total, 1 - at, 1), take(total, at, 1)
+            mine, got = mine.reshape(-1, 2, n, D), got.reshape(-1, 2, n, D)
+            self.sent = add(take(mine, 1 - at, 1), take(got, 1 - at, 1))
+            self.keep = add(take(mine, at, 1), take(got, at, 1))
             self.route = over_z(bit)
         else:
-            return total[0]
+            return add(mine, got)[0]
         self.stage += 1
         return self.sent
 
@@ -411,6 +419,25 @@
     )
 
 
+def times_transposed_kernel(left_ref, right_ref, out_ref):
+    out_ref[...] = dot_over(left_ref[...], right_ref[...], 1, 1).astype(bf16)
+
+
+def times_transposed(left, right):
+    rows, size = left.shape[0], BLOCK
+    block = pl.BlockSpec((size, D), lambda i: (i, 0))
+    return call(
+        times_transposed_kernel,
+        "times_transposed",
+        2 * rows * D * D,
+        (left, right),
+        grid=(rows // size,),
+        in_specs=[block, pl.BlockSpec((D, D), lambda i: (0, 0))],
+        out_specs=block,
+        out_shape=jax.ShapeDtypeStruct((rows, D), bf16),
+    )
+
+
 def up_kernel(second_ref, up_ref, bias_ref, active_ref, slope_ref):
     pre = dot_over(second_ref[...], up_ref[...], 1, 1) + bias_ref[...]
     root = math.sqrt(2.0 / math.pi)
@@ -666,20 +693,26 @@
     up_unit = lax.dynamic_slice_in_dim(up_weight, grid.r * n, n, 1).astype(bf16).T
     down_unit = lax.dynamic_slice_in_dim(down_weight, grid.r * n, n, 0).astype(bf16)
 
+    positions = jnp.arange(BLOCK, dtype=jnp.int32)
+    row_valid = (positions[None, :] < lengths[:, None]).astype(f32).reshape(row_count, 1)
+    grad_out = cotangent.reshape(row_count, D).astype(f32) * row_valid
+    grad_low = grad_out.astype(bf16)
+
     got, offs = gather_z(grid, attn_unit)
     attn_z = [part[:, :n] for part in got]
     small_z = jnp.concatenate([part[:, n:] for part in got])
-    up_z = gather_z(grid, after(up_unit, got[1]))[0]
+    own = small_z.reshape(grid.zs, EXTRA * D)[:, : 12 * n]
+    other = grid.move(own, over_x)
+    up_z = gather_z(grid, after(up_unit, got[1], grad_low))[0]
     attn_xy, attn_pieces = gather_rest(grid, attn_z)
-    up_held = after(jnp.concatenate(up_z), *attn_xy)
+    up_held = after(jnp.concatenate(up_z), *attn_xy, other)
     up_both = jnp.stack([up_held, grid.move(up_held, y_then_x)])
     up_late = grid.move(up_both, x_then_y)
     down_unit = after(down_unit, *attn_pieces)
     joined = [offs[0] + offs[1]]
     attn_full = assemble(grid, attn_pieces, offs, n)
 
-    own = small_z.reshape(grid.zs, EXTRA * D)[:, : 12 * n]
-    pair = jnp.stack([own, grid.move(own, over_x)])
+    pair = jnp.stack([own, other])
     pair = jnp.stack([take(pair, grid.x), take(pair, 1 - grid.x)])
     where_off = jnp.array([joined[0].index(z) for z in range(grid.zs)])
     pair = pair[:, where_off[jnp.bitwise_xor(grid.z, jnp.arange(grid.zs))]]
@@ -695,8 +728,6 @@
     out_full = attn_full[3]
 
     flat_in = hidden_in.reshape(row_count, D).astype(f32)
-    positions = jnp.arange(BLOCK, dtype=jnp.int32)
-    row_valid = (positions[None, :] < lengths[:, None]).astype(f32).reshape(row_count, 1)
     normed_one, hat_one, inv_one = norm_forward(flat_in, vec_values[0], vec_values[1])
     normed_low = normed_one.astype(bf16)
     bias_rows = jnp.stack([vec_values[2], jnp.zeros((D,), f32), vec_values[3]])
@@ -721,8 +752,6 @@
     down_both = jnp.stack([down_held, down_got])
     active_low, slope = up_forward(second_low, up_full, bias_full, [down_both])
     down_late = after(grid.move(down_both, x_then_y), active_low)
-    grad_out = cotangent.reshape(row_count, D).astype(f32) * row_valid
-    grad_low = grad_out.astype(bf16)
     down_bias_grad = jnp.sum(grad_out, axis=0)
     down_grad = weight_grad(active_low, grad_low, [down_late])
     down_pieces = [down_both, down_late] + [
@@ -730,15 +759,14 @@
     ]
     down_full = assemble(grid, down_pieces, joined, n).reshape(ff, D)
     down_sum = reduce_rows(grid, after(down_grad, *down_pieces), n)
-    down_out = jnp.dot(active_low, down_full, preferred_element_type=f32) + vec_values[7]
-    output = ((residual + down_out) * row_valid).astype(bf16).reshape(slots, BLOCK, D)
-
     up_low, upbias_grad = active_back(grad_low, down_full, slope, [down_sum.sent])
     down_sum.hold(up_low)
     down_sent = down_sum.step()
-    up_sum = reduce_rows(grid, weight_grad(up_low, second_low, [down_sent]), n)
+    up_grad = weight_grad(up_low, second_low, [down_sent])
+    down_sum.hold(up_grad)
+    up_sum = reduce_rows(grid, after(up_grad, down_sum.step()), n)
     resid_grad, branch_low, norm_sums = up_back(
-        up_low, up_full, residual, grad_low, vec_values[5], [up_sum.sent]
+        up_low, up_full, residual, grad_low, vec_values[5], [up_sum.sent, down_sum.sent]
     )
     scale_two_grad, offset_two_grad, out_bias_grad = norm_sums[0], norm_sums[1], norm_sums[2]
     for each in (down_sum, up_sum):
@@ -747,9 +775,9 @@
     out_grad = jnp.einsum(
         "nd,ne->de", context_flat, branch_low, preferred_element_type=f32
     ).astype(bf16)
-    context_grad = jnp.einsum("ne,de->nd", branch_low, out_full, preferred_element_type=f32)
+    context_grad = times_transposed(branch_low, out_full)
     rows_grad = attend_back(
-        qkv_rows, logsum, context_grad.astype(bf16), [down_sent, up_sent, out_grad]
+        qkv_rows, logsum, context_grad, [down_sent, up_sent, out_grad]
     )
     for each in (down_sum, up_sum):
         each.hold(rows_grad[0])
@@ -759,6 +787,14 @@
         for part in rows_grad
     ]
     first = grid.c == 0
+    for each in (down_sum, up_sum):
+        each.hold(value_grad)
+    if down_sum.left():
+        down_sum.step()
+        down_ready = down_sum.sent
+    else:
+        down_ready = down_unit_grad = down_sum.step()
+    value_grad = after(value_grad, up_sum.step(), down_ready)
     theirs = jnp.stack([jnp.where(first, key_grad, query_grad), jnp.where(first, out_grad, value_grad)])
     mine = jnp.stack([jnp.where(first, query_grad, key_grad), jnp.where(first, value_grad, out_grad)])
     split = (2, grid.shards, n, D)
@@ -777,23 +813,31 @@
         [first_sums[:4], out_bias_grad[None], norm_sums[:2], down_bias_grad[None]]
         + [upbias_grad.reshape(4, D)]
     )
+    small_grad = jnp.concatenate(
+        [first_sums[:4], out_bias_grad[None], norm_sums[:2], down_bias_grad[None]]
+        + [upbias_grad.reshape(4, D)]
+    )
     attn_sum.hold(first_sums)
-    waits = [output]
+    attn_sent = attn_sum.step()
+    down_out = jnp.dot(
+        after(active_low, attn_sent), down_full, preferred_element_type=f32
+    ) + vec_values[7]
+    output = ((residual + down_out) * row_valid).astype(bf16).reshape(slots, BLOCK, D)
+    up_sum.hold(attn_sent)
+    up_sum.step()
     routes = [over_core, over_y, over_x] + [over_z(bit) for bit in z_bits(grid.zs)]
-    for route in routes:
-        if attn_sum.left():
-            attn_sent = attn_sum.step()
-            for each in (up_sum, down_sum):
-                if each.left():
-                    each.hold(attn_sent)
-                    each.step()
-            if waits:
-                attn_sum.hold(*waits)
-            waits = []
-        small_grad = plain_add(small_grad, grid.move(small_grad, route), [attn_sent])
+    ties = [attn_sent]
+    for at, route in enumerate(routes):
+        if at >= 2 and attn_sum.left():
+            attn_sum.hold(output)
+            ties = [attn_sum.step()]
+        small_grad = plain_add(small_grad, grid.move(small_grad, route), ties)
+        ties = [output]
+    if down_sum.left():
+        down_unit_grad = down_sum.finish()
+    up_sum.hold(attn_sum.sent)
+    up_unit_grad = up_sum.finish()
     attn_unit_grad = attn_sum.finish()
-    down_unit_grad = down_sum.finish()
-    up_unit_grad = up_sum.finish()
     small_own = lax.dynamic_slice_in_dim(small_grad, (2 * grid.z + grid.x) * n, n, 1)
 
     down_parts = share_unit(grid, down_unit_grad)

time: 608 us -> 575 us (0.946)
  local copies, waits for them, and re-layouts: 78.3 us -> 64.1 us
  waiting for transfers between devices: 105 us -> 94.5 us
  starting transfers between devices: 55.5 us -> 47.4 us
  Pallas kernels: 220 us -> 227 us
  matrix products: 46.4 us -> 40.1 us
    convert_element_type x15 -> x18, other arithmetic: 26.1 us -> 36.9 us  [add(): return (first.astype(f32) + second.astype(f32)).astype(bf16)]
    ppermute x49, waiting for transfers between devices: 105 us -> 94.5 us  [move(): return lax.ppermute(value, AXES, pairs)]
    select_n x3 -> x1, other arithmetic: 10.7 us -> 0.66 us  [per_device(): jnp.where(first, out_grad, value_grad)]
    ppermute x49, starting transfers between devices: 55.5 us -> 47.4 us  [move(): return lax.ppermute(value, AXES, pairs)]
    pallas_call x14 -> x15, Pallas kernels: 197 us -> 205 us  [call(): pl.pallas_call(body, in_specs=list(in_specs) + [pl.BlockSpec(memory_space...]
    squeeze x13 -> x4, local copies, waits for them, and re-layouts: 22.3 us -> 18.5 us  [take(): return lax.dynamic_index_in_dim(value, at, axis, keepdims=False)]
    dot_general x2 -> x1, matrix products: 21.3 us -> 18.1 us  [per_device(): jnp.dot(after(active_low, attn_sent), down_full, preferred_element_type=f32)]
    unnamed x146 -> x148, local copies, waits for them, and re-layouts: 21.7 us -> 23.1 us
  transfers between devices with their start and end apart: 49 -> 49, of which waited for: 18 -> 19; matrix products, arithmetic and copies ran while one was open for 22% -> 24% of each run, Pallas kernels for 34% -> 40%
where the time goes in v1:
time: 575 us; the launch traced here: 564 us
  Pallas kernels  227 us (39%)
  waiting for transfers between devices  94.5 us (16%)
  other arithmetic  88.4 us (15%)
  local copies, waits for them, and re-layouts  64.1 us (11%)
  starting transfers between devices  47.4 us (8%)
  matrix products  40.1 us (7%)
    pallas_call x15, Pallas kernels, call(): pl.pallas_call(body, in_specs=list(in_specs) + [pl.BlockSpec(memory_space...  205 us
    ppermute x49, waiting for transfers between devices, move(): return lax.ppermute(value, AXES, pairs)  94.5 us
    ppermute x49, starting transfers between devices, move(): return lax.ppermute(value, AXES, pairs)  47.4 us
    convert_element_type x18, other arithmetic, add(): return (first.astype(f32) + second.astype(f32)).astype(bf16)  36.9 us
    unnamed x148, local copies, waits for them, and re-layouts  23.1 us
    pallas_call x3, Pallas kernels, assemble(): pl.pallas_call(functools.partial(assemble_kernel, grid.zs, offs), out_sha...  22.7 us
    sub x6, other arithmetic, adam_update(): weight - step_rate * (mean_hat / (jnp.sqrt(square_hat) + adam_floor) + de...  19.8 us
    squeeze x4, local copies, waits for them, and re-layouts, take(): return lax.dynamic_index_in_dim(value, at, axis, keepdims=False)  18.5 us
  transfers between devices with their start and end apart: 49, of which 19 were waited for; matrix products, arithmetic and copies ran while one was open for 24% of the time, Pallas kernels for 40%

profile of v1, /device:TPU:0, one launch (start us, length us, event | category | flops | bytes accessed | tf_op | source)
XLA Modules:
  0.0 564.1 jit_solution(17741221616266540975)
XLA Ops:
  28.2 11.5 %collective-permute-done.1 = bf16[2,144,1088]{2,1,0:T(8,128)(2,1)S(1)} collective-permute-done((bf16[2,144,1088]{2,1,0:T(8,128)(2,1)S(1)}, bf16[2,144,1088]{2,1,0:T(8,128)(2,1)S(1)}, u32[]{:S(2)}, u32[]{:S(2)}) %collective-permute-start.1) | collective-permute-done | bytes 626720 | tf_op jit(solution)/shard_map/ppermute | solution.py:51
  48.5 5.9 %collective-permute-done.5 = bf16[2,136,1088]{2,1,0:T(8,128)(2,1)S(1)} collective-permute-done((bf16[2,136,1088]{2,1,0:T(8,128)(2,1)S(1)}, bf16[2,136,1088]{2,1,0:T(8,128)(2,1)S(1)}, u32[]{:S(2)}, u32[]{:S(2)}) %collective-permute-start.5) | collective-permute-done | bytes 591904 | tf_op jit(solution)/shard_map/ppermute | solution.py:51
  60.3 13.8 %collective-permute-done.12 = bf16[2,136,1088]{2,1,0:T(8,128)(2,1)} collective-permute-done((bf16[2,136,1088]{2,1,0:T(8,128)(2,1)S(1)}, bf16[2,136,1088]{2,1,0:T(8,128)(2,1)}, u32[]{:S(2)}, u32[]{:S(2)}) %collective-permute-start.12) | collective-permute-done | bytes 591904 | tf_op jit(solution)/shard_map/ppermute | solution.py:51
  85.6 9.5 %collective-permute-done.13 = bf16[4,136,1088]{2,1,0:T(8,128)(2,1)} collective-permute-done((bf16[4,136,1088]{2,1,0:T(8,128)(2,1)S(1)}, bf16[4,136,1088]{2,1,0:T(8,128)(2,1)}, u32[]{:S(2)}, u32[]{:S(2)}) %collective-permute-start.13) | collective-permute-done | bytes 1183776 | tf_op jit(solution)/shard_map/ppermute | solution.py:51
  107.6 7.8 %assemble.3 = bf16[4,8,136,1088]{3,2,1,0:T(8,128)(2,1)} custom-call(bf16[2,2,136,1088]{3,2,1,0:T(8,128)(2,1)} %pad_maximum_fusion.4.refs_0_, bf16[2,2,136,1088]{3,2,1,0:T(8,128)(2,1)} %collective-permute-done.4.refs_1_, bf16[2,2,136,1088]{3,2,1,0:T(8,128)(2,1)} %pad_maximum_fusion.5.refs_2_, bf16[2,2,136,1088]{3,2,1,0:T(8,128)(2,1)} %collective-permute-done.6.refs_3_, ...), custom_call_target="tpu_custom_call" | custom-call | bytes 20000000 | tf_op jit(solution)/shard_map/assemble/pallas_call | solution.py:141
  115.4 14.4 %qkv_forward.1.refs_0_.refs_1_.refs_2_ = bf16[3,1024,1088]{2,1,0:T(8,128)(2,1)} custom-call(bf16[1024,1088]{1,0:T(8,128)(2,1)} %fusion.3.refs_0_, bf16[4,1088,1088]{2,1,0:T(8,128)(2,1)} %bitcast.351, f32[3,1,1088]{2,1,0:T(1,128)} %reshape.423.refs_2_, bf16[136,1088]{1,0:T(8,128)(2,1)} %dynamic-slice_convert_fusion.1.refs_3_), custom_call_target="tpu_custom_call" | custom-call | flops 7272923136 | bytes 20000000 | tf_op jit(solution)/shard_map/qkv_forward/pallas_call | solution.py:389
  133.5 23.1 %attend.1 = (bf16[1024,1088]{1,0:T(8,128)(2,1)}, f32[17,1,1024]{2,1,0:T(1,128)}) custom-call(bf16[3,1024,1088]{2,1,0:T(8,128)(2,1)} %qkv_forward.1.refs_0_.refs_1_.refs_2_, bf16[3,1024,1088]{2,1,0:T(8,128)(2,1)} %qkv_forward.1.refs_0_.refs_1_.refs_2_, bf16[3,1024,1088]{2,1,0:T(8,128)(2,1)} %qkv_forward.1.refs_0_.refs_1_.refs_2_, ...), custom_call_target="tpu_custom_call" | custom-call | flops 14000000000 | bytes 20000000 | tf_op jit(solution)/shard_map/attend/pallas_call | solution.py:389
  159.9 5.4 fusion.63
  168.3 7.4 %assemble.4 = bf16[4,8,136,1088]{3,2,1,0:T(8,128)(2,1)} custom-call(bf16[2,4,136,1088]{3,2,1,0:T(8,128)(2,1)} %copy-done.6, bf16[2,4,136,1088]{3,2,1,0:T(8,128)(2,1)} %collective-permute-done.14.refs_3_.refs_1_, bf16[2,4,136,1088]{3,2,1,0:T(8,128)(2,1)} %collective-permute-done.17.refs_2_, bf16[2,4,136,1088]{3,2,1,0:T(8,128)(2,1)} %collective-permute-done.18.refs_3_), custom_call_target="tpu_custom_call" | custom-call | bytes 20000000 | tf_op jit(solution)/shard_map/assemble/pallas_call | solution.py:141
  179.2 26.0 %up_forward.1 = (bf16[1024,4352]{1,0:T(8,128)(2,1)}, bf16[1024,4352]{1,0:T(8,128)(2,1)}) custom-call(bf16[1024,1088]{1,0:T(8,128)(2,1)} %add_convert_fusion.6.refs_0_.refs_1_, bf16[4352,1088]{1,0:T(8,128)(2,1)} %bitcast.358, f32[1,4352]{1,0:T(1,128)} %reshape.454.refs_2_, bf16[2,4,136,1088]{3,2,1,0:T(8,128)(2,1)} %copy-done.7), custom_call_target="tpu_custom_call" | custom-call | flops 9697230848 | bytes 20000000 | tf_op jit(solution)/shard_map/up_forward/pallas_call | solution.py:389
  207.9 17.3 %weight_grad.2 = bf16[4352,1088]{1,0:T(8,128)(2,1)} custom-call(bf16[1024,4352]{1,0:T(8,128)(2,1)} %get-tuple-element.118.refs_0_, bf16[1024,1088]{1,0:T(8,128)(2,1)} %fusion.5.refs_1_.refs_0_.refs_3_, bf16[2,4,136,1088]{3,2,1,0:T(8,128)(2,1)} %collective-permute-done.20.refs_2_.refs_1_), custom_call_target="tpu_custom_call" | custom-call | flops 9697230848 | bytes 20000000 | tf_op jit(solution)/shard_map/weight_grad/pallas_call | solution.py:389
  225.2 8.5 %dynamic-slice_bitcast_fusion.2 = (bf16[2,8,136,1088]{3,2,1,0:T(8,128)(2,1)}, bf16[2,8,136,1088]{3,2,1,0:T(8,128)(2,1)}) fusion(bf16[2,2,8,136,1088]{4,3,2,1,0:T(8,128)(2,1)} %bitcast.355, s32[]{:T(128)S(6)} %select_n.278, s32[]{:T(128)S(6)} %select_n.277), kind=kLoop, calls=%fused_computation.24 | loop fusion | bytes 18939912 | tf_op jit(solution)/shard_map/jit(dynamic_index_in_dim)/squeeze | solution.py:83
  234.2 7.4 %assemble.5 = bf16[4,8,136,1088]{3,2,1,0:T(8,128)(2,1)} custom-call(bf16[2,4,136,1088]{3,2,1,0:T(8,128)(2,1)} %copy-done.7, bf16[2,4,136,1088]{3,2,1,0:T(8,128)(2,1)} %collective-permute-done.20.refs_2_.refs_1_, bf16[2,4,136,1088]{3,2,1,0:T(8,128)(2,1)} %collective-permute-done.21.refs_2_, bf16[2,4,136,1088]{3,2,1,0:T(8,128)(2,1)} %collective-permute-done.22.refs_3_), custom_call_target="tpu_custom_call" | custom-call | bytes 20000000 | tf_op jit(solution)/shard_map/assemble/pallas_call | solution.py:141
  241.7 19.5 %active_back.1 = (bf16[1024,4352]{1,0:T(8,128)(2,1)}, f32[1,4352]{1,0:T(1,128)}) custom-call(bf16[1024,1088]{1,0:T(8,128)(2,1)} %fusion.5.refs_1_.refs_0_.refs_3_, bf16[4352,1088]{1,0:T(8,128)(2,1)} %bitcast.356, bf16[1024,4352]{1,0:T(8,128)(2,1)} %get-tuple-element.89.refs_2_, bf16[2,8,136,1088]{3,2,1,0:T(8,128)(2,1)} %get-tuple-element.235.refs_3_), custom_call_target="tpu_custom_call" | custom-call | flops 9697230848 | bytes 20000000 | tf_op jit(solution)/shard_map/active_back/pallas_call | solution.py:389
  266.0 5.3 add_convert_fusion.4
  271.4 17.3 %weight_grad.3 = bf16[4352,1088]{1,0:T(8,128)(2,1)} custom-call(bf16[1024,4352]{1,0:T(8,128)(2,1)} %get-tuple-element.91.refs_0_, bf16[1024,1088]{1,0:T(8,128)(2,1)} %add_convert_fusion.6.refs_0_.refs_1_, bf16[2,4,136,1088]{3,2,1,0:T(8,128)(2,1)} %copy-done.25), custom_call_target="tpu_custom_call" | custom-call | flops 9697230848 | bytes 20000000 | tf_op jit(solution)/shard_map/weight_grad/pallas_call | solution.py:389
  288.7 7.0 %collective-permute-done.24 = bf16[2,4,136,1088]{3,2,1,0:T(8,128)(2,1)} collective-permute-done((bf16[2,4,136,1088]{3,2,1,0:T(8,128)(2,1)S(1)}, bf16[2,4,136,1088]{3,2,1,0:T(8,128)(2,1)}, u32[]{:S(2)}, u32[]{:S(2)}) %collective-permute-start.24) | collective-permute-done | bytes 2367520 | tf_op jit(solution)/shard_map/ppermute | solution.py:51
  298.0 9.0 %dynamic-slice_bitcast_fusion = (bf16[2,8,136,1088]{3,2,1,0:T(8,128)(2,1)}, bf16[2,8,136,1088]{3,2,1,0:T(8,128)(2,1)}) fusion(bf16[2,2,8,136,1088]{4,3,2,1,0:T(8,128)(2,1)} %bitcast.354, s32[]{:T(128)S(6)} %select_n.278, s32[]{:T(128)S(6)} %select_n.277), kind=kLoop, calls=%fused_computation.20 | loop fusion | bytes 18939912 | tf_op jit(solution)/shard_map/jit(dynamic_index_in_dim)/squeeze | solution.py:83
  309.1 21.3 %up_back.1 = (f32[1024,1088]{1,0:T(8,128)}, bf16[1024,1088]{1,0:T(8,128)(2,1)}, f32[8,1088]{1,0:T(8,128)}) custom-call(bf16[1024,4352]{1,0:T(8,128)(2,1)} %get-tuple-element.91.refs_0_, bf16[4352,1088]{1,0:T(8,128)(2,1)} %bitcast.359, f32[1024,1088]{1,0:T(8,128)} %copy-done.5, bf16[1024,1088]{1,0:T(8,128)(2,1)} %fusion.5.refs_1_.refs_0_.refs_3_, ...), custom_call_target="tpu_custom_call" | custom-call | flops 9697230848 | bytes 20000000 | tf_op jit(solution)/shard_map/up_back/pallas_call | solution.py:389
  330.4 7.4 %times_transposed.1.refs_4_ = bf16[1024,1088]{1,0:T(8,128)(2,1)} custom-call(bf16[1024,1088]{1,0:T(8,128)(2,1)} %get-tuple-element.97.refs_0_, bf16[1088,1088]{1,0:T(8,128)(2,1)} %bitcast.378), custom_call_target="tpu_custom_call" | custom-call | flops 2424307712 | bytes 20000000 | tf_op jit(solution)/shard_map/times_transposed/pallas_call | solution.py:389
  337.8 7.0 %convolution_convert_fusion.3.refs_7_ = bf16[1088,1088]{1,0:T(8,128)(2,1)} fusion(bf16[1024,1088]{1,0:T(8,128)(2,1)} %get-tuple-element.80, bf16[1024,1088]{1,0:T(8,128)(2,1)} %get-tuple-element.97.refs_0_), kind=kOutput, calls=%fused_computation.5 | convolution fusion | flops 2425491456 | bytes 6823936 | tf_op jit(solution)/shard_map/nd,ne->de/dot_general | solution.py:775
  353.3 31.0 %attend_back.1 = (bf16[1024,1088]{1,0:T(8,128)(2,1)}, bf16[1024,1088]{1,0:T(8,128)(2,1)}, bf16[1024,1088]{1,0:T(8,128)(2,1)}) custom-call(bf16[3,1024,1088]{2,1,0:T(8,128)(2,1)} %qkv_forward.1.refs_0_.refs_1_.refs_2_, bf16[3,1024,1088]{2,1,0:T(8,128)(2,1)} %qkv_forward.1.refs_0_.refs_1_.refs_2_, bf16[3,1024,1088]{2,1,0:T(8,128)(2,1)} %qkv_forward.1.refs_0_.refs_1_.refs_2_, ...), custom_call_target="tpu_custom_call" | custom-call | flops 17999998976 | bytes 20000000 | tf_op jit(solution)/shard_map/attend_back/pallas_call | solution.py:389
  399.9 5.9 %collective-permute-done.30 = bf16[1,136,1088]{2,1,0:T(8,128)(2,1)S(1)} collective-permute-done((bf16[1,136,1088]{2,1,0:T(8,128)(2,1)S(1)}, bf16[1,136,1088]{2,1,0:T(8,128)(2,1)S(1)}, u32[]{:S(2)}, u32[]{:S(2)}) %collective-permute-start.30) | collective-permute-done | bytes 295968 | tf_op jit(solution)/shard_map/ppermute | solution.py:51
  413.7 8.3 %collective-permute-done.31 = bf16[2,8,136,1088]{3,2,1,0:T(8,128)(2,1)S(1)} collective-permute-done((bf16[2,8,136,1088]{3,2,1,0:T(8,128)(2,1)S(1)}, bf16[2,8,136,1088]{3,2,1,0:T(8,128)(2,1)S(1)}, u32[]{:S(2)}, u32[]{:S(2)}) %collective-permute-start.31) | collective-permute-done | bytes 4735008 | tf_op jit(solution)/shard_map/ppermute | solution.py:51
  431.3 19.6 %qkv_back.1 = (f32[1024,1088]{1,0:T(8,128)}, f32[8,1088]{1,0:T(8,128)}) custom-call(bf16[1024,1088]{1,0:T(8,128)(2,1)} %get-tuple-element.107.refs_0_, bf16[1024,1088]{1,0:T(8,128)(2,1)} %get-tuple-element.108.refs_1_, bf16[1024,1088]{1,0:T(8,128)(2,1)} %get-tuple-element.109.refs_2_, bf16[4,1088,1088]{2,1,0:T(8,128)(2,1)} %bitcast.352, ...), custom_call_target="tpu_custom_call" | custom-call | flops 7272923136 | bytes 20000000 | tf_op jit(solution)/shard_map/qkv_back/pallas_call | solution.py:389
  451.0 4.9 collective-permute-done.32
  459.2 18.1 %multiply_convert_fusion = bf16[1024,1088]{1,0:T(8,128)(2,1)} fusion(f32[1024,1088]{1,0:T(8,128)S(1)} %bitcast.350, bf16[1024,4352]{1,0:T(8,128)(2,1)} %get-tuple-element.118.refs_0_, bf16[4352,1088]{1,0:T(8,128)(2,1)} %bitcast.357, f32[1088]{0:T(1024)S(1)} %add.486, f32[1024]{0:T(1024)S(1)} %bitcast.395), kind=kOutput, calls=%fused_computation.33 | convolution fusion | flops 9701687296 | bytes 25075968 | tf_op jit(solution)/shard_map/dot_general | solution.py:822
  512.9 6.1 %copy.192 = f32[2,512,1088]{1,2,0:T(8,128)} copy(f32[2,512,1088]{2,1,0:T(8,128)} %bitcast.370) | data formatting | bytes 8912896
  532.5 6.8 %collective-permute-done.36 = bf16[136,1088]{1,0:T(8,128)(2,1)S(1)} collective-permute-done((bf16[136,1088]{1,0:T(8,128)(2,1)S(1)}, bf16[136,1088]{1,0:T(8,128)(2,1)S(1)}, u32[]{:S(2)}, u32[]{:S(2)}) %collective-permute-start.36) | collective-permute-done | bytes 295968 | tf_op jit(solution)/shard_map/ppermute | solution.py:51
  542.8 5.4 multiply_subtract_fusion
  548.2 5.4 multiply_subtract_fusion.1
  558.3 5.4 multiply_subtract_fusion.2
  (364 shorter events, 193.2 us)
Async XLA Ops:
  4.4 19.0 %collective-permute-start = (bf16[1,144,1088]{2,1,0:T(8,128)(2,1)S(1)}, bf16[1,144,1088]{2,1,0:T(8,128)(2,1)S(1)}, u32[]{:S(2)}, u32[]{:S(2)}) collective-permute-start(bf16[1,144,1088]{2,1,0:T(8,128)(2,1)S(1)} %maximum_bitcast_fusion), channel_id=1, source_target_pairs={{0,16},{1,17},{2,18},{3,19},{4,20},{5,21},{6,22},{7,23},{8,24},{9,... | collective-permute-start | bytes 940040 | tf_op jit(solution)/shard_map/ppermute | solution.py:51
  23.5 16.2 %collective-permute-start.1 = (bf16[2,144,1088]{2,1,0:T(8,128)(2,1)S(1)}, bf16[2,144,1088]{2,1,0:T(8,128)(2,1)S(1)}, u32[]{:S(2)}, u32[]{:S(2)}) collective-permute-start(bf16[2,144,1088]{2,1,0:T(8,128)(2,1)S(1)} %pad_maximum_fusion.13), channel_id=1, source_target_pairs={{0,8},{1,9},{2,10},{3,11},{4,12},{5,13},{6,14},{7,15},{8,0},{9,1},... | collective-permute-start | bytes 1880072 | tf_op jit(solution)/shard_map/ppermute | solution.py:51
  25.6 20.2 %collective-permute-start.3 = (bf16[2,136,1088]{2,1,0:T(8,128)(2,1)S(1)}, bf16[2,136,1088]{2,1,0:T(8,128)(2,1)S(1)}, u32[]{:S(2)}, u32[]{:S(2)}) collective-permute-start(bf16[2,136,1088]{2,1,0:T(8,128)(2,1)S(1)} %fusion.24), channel_id=1, source_target_pairs={{0,2},{1,5},{2,0},{3,7},{4,6},{5,1},{6,4},{7,3},{8,10},{9,13},{10,... | collective-permute-start | bytes 1775624 | tf_op jit(solution)/shard_map/ppermute | solution.py:51
  47.0 30.9 %collective-permute-start.4 = (bf16[2,2,136,1088]{3,2,1,0:T(8,128)(2,1)}, bf16[2,2,136,1088]{3,2,1,0:T(8,128)(2,1)}, u32[]{:S(2)}, u32[]{:S(2)}) collective-permute-start(bf16[2,2,136,1088]{3,2,1,0:T(8,128)(2,1)} %pad_maximum_fusion.4.refs_0_), channel_id=1, source_target_pairs={{0,4},{1,3},{2,6},{3,1},{4,0},{5,7},{6,2},{7,5},{8,12},{9,11},{10,... | collective-permute-start | bytes 3551240 | tf_op jit(solution)/shard_map/ppermute | solution.py:51
  55.6 22.3 %collective-permute-start.6 = (bf16[2,2,136,1088]{3,2,1,0:T(8,128)(2,1)}, bf16[2,2,136,1088]{3,2,1,0:T(8,128)(2,1)}, u32[]{:S(2)}, u32[]{:S(2)}) collective-permute-start(bf16[2,2,136,1088]{3,2,1,0:T(8,128)(2,1)} %pad_maximum_fusion.5.refs_2_), channel_id=1, source_target_pairs={{0,4},{1,3},{2,6},{3,1},{4,0},{5,7},{6,2},{7,5},{8,12},{9,11},{10,... | collective-permute-start | bytes 3551240 | tf_op jit(solution)/shard_map/ppermute | solution.py:51
  59.7 18.2 %collective-permute-start.2 = (bf16[4,1632]{1,0:T(4,128)(2,1)S(1)}, bf16[4,1632]{1,0:T(4,128)(2,1)S(1)}, u32[]{:S(2)}, u32[]{:S(2)}) collective-permute-start(bf16[4,1632]{1,0:T(4,128)(2,1)S(1)} %get-tuple-element.281), channel_id=1, source_target_pairs={{0,4},{1,5},{2,6},{3,7},{4,0},{5,1},{6,2},{7,3},{8,12},{9,13},{10,... | collective-permute-start | bytes 39176 | tf_op jit(solution)/shard_map/ppermute | solution.py:51
  77.9 17.1 %collective-permute-start.13 = (bf16[4,136,1088]{2,1,0:T(8,128)(2,1)S(1)}, bf16[4,136,1088]{2,1,0:T(8,128)(2,1)}, u32[]{:S(2)}, u32[]{:S(2)}) collective-permute-start(bf16[4,136,1088]{2,1,0:T(8,128)(2,1)S(1)} %pad_maximum_fusion.6), channel_id=1, source_target_pairs={{0,2},{1,5},{2,0},{3,7},{4,6},{5,1},{6,4},{7,3},{8,10},{9,13},{10,... | collective-permute-start | bytes 3551240 | tf_op jit(solution)/shard_map/ppermute | solution.py:51
  84.1 21.3 %collective-permute-start.7 = (bf16[2,2,136,1088]{3,2,1,0:T(8,128)(2,1)}, bf16[2,2,136,1088]{3,2,1,0:T(8,128)(2,1)}, u32[]{:S(2)}, u32[]{:S(2)}) collective-permute-start(bf16[2,2,136,1088]{3,2,1,0:T(8,128)(2,1)} %pad_maximum_fusion.4.refs_0_), channel_id=1, source_target_pairs={{0,1},{1,0},{2,3},{3,2},{4,5},{5,4},{6,7},{7,6},{8,9},{9,8},{10,11... | collective-permute-start | bytes 3551240 | tf_op jit(solution)/shard_map/ppermute | solution.py:51
  97.0 36.5 %collective-permute-start.14 = (bf16[2,4,136,1088]{3,2,1,0:T(8,128)(2,1)S(1)}, bf16[2,4,136,1088]{3,2,1,0:T(8,128)(2,1)}, u32[]{:S(2)}, u32[]{:S(2)}) collective-permute-start(bf16[2,4,136,1088]{3,2,1,0:T(8,128)(2,1)S(1)} %pad_maximum_fusion.2.refs_0_), channel_id=1, source_target_pairs={{0,4},{1,3},{2,6},{3,1},{4,0},{5,7},{6,2},{7,5},{8,12},{9,11},{10,... | collective-permute-start | bytes 7102472 | tf_op jit(solution)/shard_map/ppermute | solution.py:51
  105.3 54.5 %collective-permute-start.17 = (bf16[2,4,136,1088]{3,2,1,0:T(8,128)(2,1)S(1)}, bf16[2,4,136,1088]{3,2,1,0:T(8,128)(2,1)}, u32[]{:S(2)}, u32[]{:S(2)}) collective-permute-start(bf16[2,4,136,1088]{3,2,1,0:T(8,128)(2,1)S(1)} %pad_maximum_fusion.2.refs_0_), channel_id=1, source_target_pairs={{0,1},{1,0},{2,3},{3,2},{4,5},{5,4},{6,7},{7,6},{8,9},{9,8},{10,11... | collective-permute-start | bytes 7102472 | tf_op jit(solution)/shard_map/ppermute | solution.py:51
  105.8 26.0 %collective-permute-start.15 = (bf16[1,136,1088]{2,1,0:T(8,128)(2,1)S(1)}, bf16[1,136,1088]{2,1,0:T(8,128)(2,1)S(1)}, u32[]{:S(2)}, u32[]{:S(2)}) collective-permute-start(bf16[1,136,1088]{2,1,0:T(8,128)(2,1)S(1)} %bitcast.371), channel_id=1, source_target_pairs={{0,16},{1,17},{2,18},{3,19},{4,20},{5,21},{6,22},{7,23},{8,24},{9,... | collective-permute-start | bytes 887816 | tf_op jit(solution)/shard_map/ppermute | solution.py:51
  131.9 24.8 %collective-permute-start.16 = (bf16[2,136,1088]{2,1,0:T(8,128)(2,1)S(1)}, bf16[2,136,1088]{2,1,0:T(8,128)(2,1)S(1)}, u32[]{:S(2)}, u32[]{:S(2)}) collective-permute-start(bf16[2,136,1088]{2,1,0:T(8,128)(2,1)S(1)} %pad_maximum_fusion.15.refs_4_), channel_id=1, source_target_pairs={{0,8},{1,9},{2,10},{3,11},{4,12},{5,13},{6,14},{7,15},{8,0},{9,1},... | collective-permute-start | bytes 1775624 | tf_op jit(solution)/shard_map/ppermute | solution.py:51
  158.0 17.7 %collective-permute-start.19 = (bf16[4,136,1088]{2,1,0:T(8,128)(2,1)}, bf16[4,136,1088]{2,1,0:T(8,128)(2,1)}, u32[]{:S(2)}, u32[]{:S(2)}) collective-permute-start(bf16[4,136,1088]{2,1,0:T(8,128)(2,1)} %get-tuple-element.271), channel_id=1, source_target_pairs={{0,2},{1,5},{2,0},{3,7},{4,6},{5,1},{6,4},{7,3},{8,10},{9,13},{10,... | collective-permute-start | bytes 3551240 | tf_op jit(solution)/shard_map/ppermute | solution.py:51
  177.3 30.6 %collective-permute-start.20 = (bf16[2,4,136,1088]{3,2,1,0:T(8,128)(2,1)S(1)}, bf16[2,4,136,1088]{3,2,1,0:T(8,128)(2,1)}, u32[]{:S(2)}, u32[]{:S(2)}) collective-permute-start(bf16[2,4,136,1088]{3,2,1,0:T(8,128)(2,1)S(1)} %pad_maximum_fusion.3.refs_3_.refs_0_), channel_id=1, source_target_pairs={{0,4},{1,3},{2,6},{3,1},{4,0},{5,7},{6,2},{7,5},{8,12},{9,11},{10,... | collective-permute-start | bytes 7102472 | tf_op jit(solution)/shard_map/ppermute | solution.py:51
  179.2 45.9 %collective-permute-start.21 = (bf16[2,4,136,1088]{3,2,1,0:T(8,128)(2,1)S(1)}, bf16[2,4,136,1088]{3,2,1,0:T(8,128)(2,1)}, u32[]{:S(2)}, u32[]{:S(2)}) collective-permute-start(bf16[2,4,136,1088]{3,2,1,0:T(8,128)(2,1)S(1)} %pad_maximum_fusion.3.refs_3_.refs_0_), channel_id=1, source_target_pairs={{0,1},{1,0},{2,3},{3,2},{4,5},{5,4},{6,7},{7,6},{8,9},{9,8},{10,11... | collective-permute-start | bytes 7102472 | tf_op jit(solution)/shard_map/ppermute | solution.py:51
  207.9 17.3 %collective-permute-start.22 = (bf16[2,4,136,1088]{3,2,1,0:T(8,128)(2,1)}, bf16[2,4,136,1088]{3,2,1,0:T(8,128)(2,1)}, u32[]{:S(2)}, u32[]{:S(2)}) collective-permute-start(bf16[2,4,136,1088]{3,2,1,0:T(8,128)(2,1)} %collective-permute-done.20.refs_2_.refs_1_), channel_id=1, source_target_pairs={{0,1},{1,0},{2,3},{3,2},{4,5},{5,4},{6,7},{7,6},{8,9},{9,8},{10,11... | collective-permute-start | bytes 7102472 | tf_op jit(solution)/shard_map/ppermute | solution.py:51
  233.7 27.5 %collective-permute-start.23 = (bf16[2,8,136,1088]{3,2,1,0:T(8,128)(2,1)}, bf16[2,8,136,1088]{3,2,1,0:T(8,128)(2,1)}, u32[]{:S(2)}, u32[]{:S(2)}) collective-permute-start(bf16[2,8,136,1088]{3,2,1,0:T(8,128)(2,1)} %get-tuple-element.235.refs_3_), channel_id=1, source_target_pairs={{0,1},{1,0},{2,3},{3,2},{4,5},{5,4},{6,7},{7,6},{8,9},{9,8},{10,11... | collective-permute-start | bytes 14204936 | tf_op jit(solution)/shard_map/ppermute | solution.py:51
  265.0 30.6 %collective-permute-start.24 = (bf16[2,4,136,1088]{3,2,1,0:T(8,128)(2,1)S(1)}, bf16[2,4,136,1088]{3,2,1,0:T(8,128)(2,1)}, u32[]{:S(2)}, u32[]{:S(2)}) collective-permute-start(bf16[2,4,136,1088]{3,2,1,0:T(8,128)(2,1)S(1)} %add_convert_fusion.5.refs_2_), channel_id=1, source_target_pairs={{0,4},{1,3},{2,6},{3,1},{4,0},{5,7},{6,2},{7,5},{8,12},{9,11},{10,... | collective-permute-start | bytes 7102472 | tf_op jit(solution)/shard_map/ppermute | solution.py:51
  307.0 41.1 %collective-permute-start.26 = (bf16[2,8,136,1088]{3,2,1,0:T(8,128)(2,1)}, bf16[2,8,136,1088]{3,2,1,0:T(8,128)(2,1)}, u32[]{:S(2)}, u32[]{:S(2)}) collective-permute-start(bf16[2,8,136,1088]{3,2,1,0:T(8,128)(2,1)} %get-tuple-element.233.refs_5_), channel_id=1, source_target_pairs={{0,1},{1,0},{2,3},{3,2},{4,5},{5,4},{6,7},{7,6},{8,9},{9,8},{10,11... | collective-permute-start | bytes 14204936 | tf_op jit(solution)/shard_map/ppermute | solution.py:51
  307.7 37.2 %collective-permute-start.25 = (bf16[4,136,1088]{2,1,0:T(8,128)(2,1)S(1)}, bf16[4,136,1088]{2,1,0:T(8,128)(2,1)}, u32[]{:S(2)}, u32[]{:S(2)}) collective-permute-start(bf16[4,136,1088]{2,1,0:T(8,128)(2,1)S(1)} %get-tuple-element.245.refs_6_), channel_id=1, source_target_pairs={{0,2},{1,5},{2,0},{3,7},{4,6},{5,1},{6,4},{7,3},{8,10},{9,13},{10,... | collective-permute-start | bytes 3551240 | tf_op jit(solution)/shard_map/ppermute | solution.py:51
  347.2 40.8 %collective-permute-start.28 = (bf16[2,136,1088]{2,1,0:T(8,128)(2,1)}, bf16[2,136,1088]{2,1,0:T(8,128)(2,1)}, u32[]{:S(2)}, u32[]{:S(2)}) collective-permute-start(bf16[2,136,1088]{2,1,0:T(8,128)(2,1)} %get-tuple-element.251.refs_5_), channel_id=1, source_target_pairs={{0,8},{1,9},{2,10},{3,11},{4,12},{5,13},{6,14},{7,15},{8,0},{9,1},... | collective-permute-start | bytes 1775624 | tf_op jit(solution)/shard_map/ppermute | solution.py:51
  351.9 37.6 %collective-permute-start.27 = (bf16[2,4,136,1088]{3,2,1,0:T(8,128)(2,1)S(1)}, bf16[2,4,136,1088]{3,2,1,0:T(8,128)(2,1)}, u32[]{:S(2)}, u32[]{:S(2)}) collective-permute-start(bf16[2,4,136,1088]{3,2,1,0:T(8,128)(2,1)S(1)} %add_convert_fusion.3.refs_6_), channel_id=1, source_target_pairs={{0,4},{1,3},{2,6},{3,1},{4,0},{5,7},{6,2},{7,5},{8,12},{9,11},{10,... | collective-permute-start | bytes 7102472 | tf_op jit(solution)/shard_map/ppermute | solution.py:51
  389.3 16.6 %collective-permute-start.30 = (bf16[1,136,1088]{2,1,0:T(8,128)(2,1)S(1)}, bf16[1,136,1088]{2,1,0:T(8,128)(2,1)S(1)}, u32[]{:S(2)}, u32[]{:S(2)}) collective-permute-start(bf16[1,136,1088]{2,1,0:T(8,128)(2,1)S(1)} %get-tuple-element.269), channel_id=1, source_target_pairs={{0,16},{1,17},{2,18},{3,19},{4,20},{5,21},{6,22},{7,23},{8,24},{9,... | collective-permute-start | bytes 887816 | tf_op jit(solution)/shard_map/ppermute | solution.py:51
  392.0 17.3 %collective-permute-start.29 = (bf16[4,136,1088]{2,1,0:T(8,128)(2,1)S(1)}, bf16[4,136,1088]{2,1,0:T(8,128)(2,1)S(1)}, u32[]{:S(2)}, u32[]{:S(2)}) collective-permute-start(bf16[4,136,1088]{2,1,0:T(8,128)(2,1)S(1)} %get-tuple-element.243), channel_id=1, source_target_pairs={{0,2},{1,5},{2,0},{3,7},{4,6},{5,1},{6,4},{7,3},{8,10},{9,13},{10,... | collective-permute-start | bytes 3551240 | tf_op jit(solution)/shard_map/ppermute | solution.py:51
  425.1 30.7 %collective-permute-start.32 = (bf16[2,4,136,1088]{3,2,1,0:T(8,128)(2,1)}, bf16[2,4,136,1088]{3,2,1,0:T(8,128)(2,1)}, u32[]{:S(2)}, u32[]{:S(2)}) collective-permute-start(bf16[2,4,136,1088]{3,2,1,0:T(8,128)(2,1)} %add_convert_fusion.1.refs_7_), channel_id=1, source_target_pairs={{0,4},{1,3},{2,6},{3,1},{4,0},{5,7},{6,2},{7,5},{8,12},{9,11},{10,... | collective-permute-start | bytes 7102472 | tf_op jit(solution)/shard_map/ppermute | solution.py:51
  426.8 59.3 %collective-permute-start.38 = (bf16[2,136,1088]{2,1,0:T(8,128)(2,1)}, bf16[2,136,1088]{2,1,0:T(8,128)(2,1)}, u32[]{:S(2)}, u32[]{:S(2)}) collective-permute-start(bf16[2,136,1088]{2,1,0:T(8,128)(2,1)} %get-tuple-element.247), channel_id=1, source_target_pairs={{0,8},{1,9},{2,10},{3,11},{4,12},{5,13},{6,14},{7,15},{8,0},{9,1},... | collective-permute-start | bytes 1775624 | tf_op jit(solution)/shard_map/ppermute | solution.py:51
  458.2 19.2 %collective-permute-start.33 = (bf16[4,136,1088]{2,1,0:T(8,128)(2,1)S(1)}, bf16[4,136,1088]{2,1,0:T(8,128)(2,1)S(1)}, u32[]{:S(2)}, u32[]{:S(2)}) collective-permute-start(bf16[4,136,1088]{2,1,0:T(8,128)(2,1)S(1)} %get-tuple-element.237.refs_2_), channel_id=1, source_target_pairs={{0,2},{1,5},{2,0},{3,7},{4,6},{5,1},{6,4},{7,3},{8,10},{9,13},{10,... | collective-permute-start | bytes 3551240 | tf_op jit(solution)/shard_map/ppermute | solution.py:51
  477.8 24.8 %collective-permute-start.34 = (bf16[2,136,1088]{2,1,0:T(8,128)(2,1)S(1)}, bf16[2,136,1088]{2,1,0:T(8,128)(2,1)S(1)}, u32[]{:S(2)}, u32[]{:S(2)}) collective-permute-start(bf16[2,136,1088]{2,1,0:T(8,128)(2,1)S(1)} %get-tuple-element.249.refs_2_), channel_id=1, source_target_pairs={{0,8},{1,9},{2,10},{3,11},{4,12},{5,13},{6,14},{7,15},{8,0},{9,1},... | collective-permute-start | bytes 1775624 | tf_op jit(solution)/shard_map/ppermute | solution.py:51
  487.4 16.9 %collective-permute-start.39 = (bf16[1,136,1088]{2,1,0:T(8,128)(2,1)S(1)}, bf16[1,136,1088]{2,1,0:T(8,128)(2,1)S(1)}, u32[]{:S(2)}, u32[]{:S(2)}) collective-permute-start(bf16[1,136,1088]{2,1,0:T(8,128)(2,1)S(1)} %get-tuple-element.264), channel_id=1, source_target_pairs={{0,16},{1,17},{2,18},{3,19},{4,20},{5,21},{6,22},{7,23},{8,24},{9,... | collective-permute-start | bytes 887816 | tf_op jit(solution)/shard_map/ppermute | solution.py:51
  504.4 22.8 %collective-permute-start.40 = (bf16[136,1088]{1,0:T(8,128)(2,1)S(1)}, bf16[136,1088]{1,0:T(8,128)(2,1)}, u32[]{:S(2)}, u32[]{:S(2)}) collective-permute-start(bf16[136,1088]{1,0:T(8,128)(2,1)S(1)} %bitcast.382), channel_id=1, source_target_pairs={{0,2},{1,3},{2,0},{3,1},{4,6},{5,7},{6,4},{7,5},{8,10},{9,11},{10,... | collective-permute-start | bytes 887816 | tf_op jit(solution)/shard_map/ppermute | solution.py:51
  505.4 22.9 %collective-permute-start.35 = (bf16[1,136,1088]{2,1,0:T(8,128)(2,1)}, bf16[1,136,1088]{2,1,0:T(8,128)(2,1)}, u32[]{:S(2)}, u32[]{:S(2)}) collective-permute-start(bf16[1,136,1088]{2,1,0:T(8,128)(2,1)} %add_convert_fusion.23.refs_2_), channel_id=1, source_target_pairs={{0,16},{1,17},{2,18},{3,19},{4,20},{5,21},{6,22},{7,23},{8,24},{9,... | collective-permute-start | bytes 887816 | tf_op jit(solution)/shard_map/ppermute | solution.py:51
  508.7 15.4 %collective-permute-start.48 = (f32[12,1088]{1,0:T(8,128)}, f32[12,1088]{1,0:T(8,128)S(1)}, u32[]{:S(2)}, u32[]{:S(2)}) collective-permute-start(f32[12,1088]{1,0:T(8,128)} %plain_add.8.refs_0_), channel_id=1, source_target_pairs={{0,16},{1,17},{2,18},{3,19},{4,20},{5,21},{6,22},{7,23},{8,24},{9,... | collective-permute-start | bytes 156680 | tf_op jit(solution)/shard_map/ppermute | solution.py:51
  (89 other events, 697.7 us)
